TPU v7x, 256 devices: a whole 4x4x8 slice. The times are simulated.
256 devices in a mesh: dp: 8 (over y, core), expert: 32 (over z, x).
Axes of the slice: x: 4, y: 4, z: 8, core: 2. Of those that a mesh axis runs over, the one named last changes fastest.
Arguments:
- tokens: bfloat16 [73728, 2048], P(('dp', 'expert')), may hold values from -36 to 36
- cotangent: bfloat16 [73728, 2048], P(('dp', 'expert')), may hold values from -1.796875 to 1.796875
- expert_ids: int32 [24576, 2], P(('dp', 'expert')), may hold values from 0 to 31, all different within a row; in each aligned block of 96 rows (0 to 95, 96 to 191, ...) at most 12 rows name the same one
- votes: int32 [24576, 2], P(('dp', 'expert')), may hold values from 1 to 8
- pool_weight: float32 [3, 2048], replicated, may hold values from 0.2 to 1
- norm_gain: float32 [2048], replicated, may hold values from 0.5 to 2
- up_gain: float32 [3, 2048], replicated, may hold values from 0.5 to 1.5
- gate_weight: bfloat16 [32, 1024, 2048], P('expert', 'dp'), may hold values from -0.125 to 0.125
- up_weight: bfloat16 [32, 1024, 2048], P('expert', 'dp'), may hold values from -0.125 to 0.125
- down_weight: bfloat16 [32, 1024, 2048], P('expert', 'dp'), may hold values from -0.1875 to 0.1875
Outputs:
- layer_out: bfloat16 [73728, 2048], P(('dp', 'expert'))
- tokens_grad: bfloat16 [73728, 2048], P(('dp', 'expert'))
- gate_grad: float32 [32, 1024, 2048], P('expert', 'dp')
- up_grad: float32 [32, 1024, 2048], P('expert', 'dp')
- down_grad: float32 [32, 1024, 2048], P('expert', 'dp')
Inputs may be any that keep to these rules, and one draw needn't show every extreme that they name: `expert_ids`: each row names 2 different experts. In every aligned block of 96 rows (the rows of one device) no expert is named by more than 12 rows, a bound that some block reaches.
All inputs are finite; a program needn't handle non-finite values.
Results may differ from a plain program's by a relative error of at most 0.015.
Values may be sent and summed in bfloat16 or wider, within the bound.
No kernel may reach another device: no remote copies, remote signals or barrier semaphores. Data moves between devices by JAX's collectives and lax.ppermute only.
A program may use at most 128 MiB of HBM per device.

v0:
```python
import functools

import jax
import jax.numpy as jnp
from jax import lax
from jax.experimental import pallas as pl
from jax.experimental.pallas import tpu as pltpu
from jax.sharding import PartitionSpec as P

BF = jnp.bfloat16
F32 = jnp.float32
MIB = 1024 * 1024
EDGE_LIMIT = 60 * MIB
AFTER_LIMIT = 52 * MIB
EXPERTS_LIMIT = 51 * MIB
SUMS_LIMIT = 60 * MIB


def nn(a, b):
    return jnp.dot(a, b, preferred_element_type=F32)


def nt(a, b):
    return lax.dot_general(a, b, (((1,), (1,)), ((), ())), preferred_element_type=F32)


def tn(a, b):
    return lax.dot_general(a, b, (((0,), (0,)), ((), ())), preferred_element_type=F32)


def iota(shape, axis):
    return lax.broadcasted_iota(jnp.int32, shape, axis)


def slots_and_gates(ids_ref, votes_ref, experts, capacity):
    rows = ids_ref.shape[1]
    ids = ids_ref[...].astype(F32).T.astype(jnp.int32)
    first, second = ids[:, 0:1], ids[:, 1:2]
    names = iota((rows, experts), 1)
    hot0 = (names == first).astype(F32)
    hot1 = (names == second).astype(F32)
    earlier = (iota((rows, rows), 0) > iota((rows, rows), 1)).astype(BF)
    before = nn(earlier, (hot0 + hot1).astype(BF))
    rank0 = jnp.sum(before * hot0, axis=1, keepdims=True).astype(jnp.int32)
    rank1 = jnp.sum(before * hot1, axis=1, keepdims=True).astype(jnp.int32)
    votes = votes_ref[...].astype(F32).T
    total = votes[:, 0:1] + votes[:, 1:2]
    slot0 = first * (2 * capacity) + rank0
    slot1 = second * (2 * capacity) + rank1
    return slot0, slot1, votes[:, 0:1] / total, votes[:, 1:2] / total


def pick(rows, factor, j):
    shape = (rows, rows * factor)
    return (iota(shape, 1) == iota(shape, 0) * factor + j).astype(BF)


def pack_kernel(w_gate, w_up, w_down, first, second, held, in_sem, out_sem):
    width = w_gate.shape[1]
    half = first.shape[0]
    loads = [pltpu.make_async_copy(src.at[0], held.at[pl.ds(m * width, width)], in_sem.at[m]) for m, src in enumerate((w_gate, w_up, w_down))]
    stores = [pltpu.make_async_copy(held.at[pl.ds(h * half, half)], dst, out_sem.at[h]) for h, dst in enumerate((first, second))]
    for copy in loads:
        copy.start()
    for copy in loads[:2]:
        copy.wait()
    stores[0].start()
    loads[2].wait()
    stores[1].start()
    for copy in stores:
        copy.wait()


def before_kernel(experts, capacity, tokens, cotangent, ids, votes, pool, norm, gain, send, scaled_out, notes):
    rows = ids.shape[1]
    factor = tokens.shape[0] // rows
    slot0, slot1, gate0, gate1 = slots_and_gates(ids, votes, experts, capacity)
    band = rows // 3
    sel = jnp.concatenate([pick(band, factor, j) for j in range(factor)], axis=0)
    shorts, mixes = [], []
    for i in range(3):
        at = slice(i * band * factor, (i + 1) * band * factor)
        tok, cot = nn(sel, tokens[at, :]), nn(sel, cotangent[at, :])
        short = d_mix = None
        for j in range(factor):
            a = tok[j * band : (j + 1) * band] * pool[j : j + 1, :]
            b = cot[j * band : (j + 1) * band] * gain[j : j + 1, :]
            short = a if short is None else short + a
            d_mix = b if d_mix is None else d_mix + b
        shorts.append(short)
        mixes.append(d_mix)
    short = jnp.concatenate(shorts, axis=0)
    d_mix = jnp.concatenate(mixes, axis=0)
    inv = lax.rsqrt(jnp.mean(short * short, axis=1, keepdims=True) + 1e-06)
    scaled = short * inv
    scaled_out[...] = scaled
    lane = iota(notes.shape, 1)
    noted = inv
    for n, column in enumerate((slot0.astype(F32), slot1.astype(F32), gate0, gate1)):
        noted = jnp.where(lane == n + 1, column, noted)
    notes[...] = noted
    values = jnp.concatenate(
        [
            (scaled * norm[...]).astype(BF),
            (gate0 * d_mix).astype(BF),
            (gate1 * d_mix).astype(BF),
        ],
        axis=0,
    )
    place = iota((rows, send.shape[0]), 1)
    spread = jnp.concatenate(
        [
            jnp.where((place == slot0) | (place == slot1), 1.0, 0.0).astype(BF),
            jnp.where(place == slot0 + capacity, 1.0, 0.0).astype(BF),
            jnp.where(place == slot1 + capacity, 1.0, 0.0).astype(BF),
        ],
        axis=0,
    )
    send[...] = tn(spread, values).astype(BF)


def split_matrix(rows, capacity):
    half = rows // 2
    r = iota((rows, rows), 0)
    c = iota((rows, rows), 1)
    kind = (r >= half).astype(jnp.int32)
    within = r - kind * half
    sender = ((within.astype(F32) + 0.5) * (1.0 / capacity)).astype(jnp.int32)
    source = within + (sender + kind) * capacity
    return (c == source).astype(BF)


def experts_kernel(capacity, group, cols, arrived, *refs):
    halves, refs = refs[:16], refs[16:]
    back, packed, left_out, mixed, w, xs, gs, acts, lefts, in_sem, w_sem, out_sem, back_sem = refs
    half = group // 2
    groups = arrived.shape[0] // group
    pieces, three, model = w.shape
    width = three // 3
    full = pieces * width
    parts = 4
    step = parts * width
    loads = [
        pltpu.make_async_copy(arrived.at[pl.ds(i * group, group)], mixed.at[pl.ds(i * group, group)], in_sem.at[i])
        for i in range(groups)
    ]
    held = [
        pltpu.make_async_copy(src, w.at[i // 2, pl.ds((i % 2) * (three // 2), three // 2)], w_sem.at[i]) for i, src in enumerate(halves)
    ]
    chunk = 2 * parts
    for copy in loads + held[:chunk]:
        copy.start()
    sel = split_matrix(group, capacity)
    for i in range(groups):
        loads[i].wait()
        if i == 1:
            for copy in held[chunk : 2 * chunk]:
                copy.start()
        both = nn(sel, mixed[i * group : (i + 1) * group, :]).astype(BF)
        xs[i * half : (i + 1) * half, :] = both[:half]
        gs[i * half : (i + 1) * half, :] = both[half:]
    outs = [pltpu.make_async_copy(src, packed.at[:, pl.ds(i * model, model)], out_sem.at[i]) for i, src in enumerate((xs, gs))]
    for c in range(pieces // parts):
        for copy in held[c * chunk : (c + 1) * chunk]:
            copy.wait()
        if c == 0:
            for copy in outs:
                copy.start()
        for copy in held[(c + 2) * chunk : (c + 3) * chunk]:
            copy.start()
        mine = slice(c * parts, (c + 1) * parts)
        x = xs[...]
        pre_gate = nt(x, w[mine, 0:width].reshape(step, model))
        pre_up = nt(x, w[mine, width : 2 * width].reshape(step, model))
        d_hidden = nt(gs[...], w[mine, 2 * width :].reshape(step, model))
        sig = jax.nn.sigmoid(pre_gate)
        active = pre_gate * sig
        hidden = active * pre_up
        d_gate = d_hidden * pre_up * sig * (1.0 + pre_gate * (1.0 - sig))
        d_up = d_hidden * active
        at = slice(c * step, (c + 1) * step)
        for m, part in enumerate((d_gate, d_up, hidden)):
            rounded = part.astype(BF)
            acts[m, :, at] = rounded
            if 2 * c < pieces // parts:
                lefts[m, at, :] = rounded.T
    mine = full // 2
    last = [pltpu.make_async_copy(lefts, left_out, out_sem.at[2])]
    for m in range(3):
        theirs = packed.at[:, pl.ds(2 * model + m * mine, mine)]
        last.append(pltpu.make_async_copy(acts.at[m, :, pl.ds(mine, mine)], theirs, out_sem.at[3 + m]))
    for copy in last:
        copy.start()
    outs += last
    for n in range(model // cols):
        at = slice(n * cols, (n + 1) * cols)
        y = nn(acts[2], w[:, 2 * width :, at].reshape(full, cols)).astype(BF)
        dx = nn(acts[0], w[:, 0:width, at].reshape(full, cols)) + nn(acts[1], w[:, width : 2 * width, at].reshape(full, cols))
        dx = dx.astype(BF)
        for i in range(groups):
            both = jnp.concatenate([y[i * half : (i + 1) * half], dx[i * half : (i + 1) * half]], axis=0)
            mixed[i * group : (i + 1) * group, at] = tn(sel, both).astype(BF)
        copy = pltpu.make_async_copy(mixed.at[:, pl.ds(n * cols, cols)], back.at[:, pl.ds(n * cols, cols)], back_sem.at[n])
        copy.start()
        outs.append(copy)
    for copy in outs:
        copy.wait()


def experts_call(arrived, halves, capacity):
    slots, width = arrived.shape
    three = 2 * halves[0].shape[0]
    pieces = len(halves) // 2
    full = pieces * three // 3
    rows = slots // 2
    group = 16 * capacity
    cols = width // 2
    hbm = pl.BlockSpec(memory_space=pl.ANY)
    return pl.pallas_call(
        functools.partial(experts_kernel, capacity, group, cols),
        in_specs=[hbm] * (1 + len(halves)),
        out_specs=[hbm] * 3,
        out_shape=(
            jax.ShapeDtypeStruct((slots, width), BF),
            jax.ShapeDtypeStruct((rows, 2 * width + 3 * full // 2), BF),
            jax.ShapeDtypeStruct((3, full // 2, rows), BF),
        ),
        scratch_shapes=[
            pltpu.VMEM((slots, width), BF),
            pltpu.VMEM((pieces, three, width), BF),
            pltpu.VMEM((rows, width), BF),
            pltpu.VMEM((rows, width), BF),
            pltpu.VMEM((3, rows, full), BF),
            pltpu.VMEM((3, full // 2, rows), BF),
            pltpu.SemaphoreType.DMA((slots // group,)),
            pltpu.SemaphoreType.DMA((len(halves),)),
            pltpu.SemaphoreType.DMA((6,)),
            pltpu.SemaphoreType.DMA((width // cols,)),
        ],
        compiler_params=pltpu.CompilerParams(vmem_limit_bytes=EXPERTS_LIMIT),
        cost_estimate=pl.CostEstimate(flops=12 * rows * full * width, bytes_accessed=8 * slots * width, transcendentals=rows * full),
        name="experts",
    )(arrived, *halves)


def sums_kernel(jobs, packed_a, left_a, packed_b, d0, d1, d2, d3, x, g, left, acts, p, in_sem, out_sem):
    rows = left_a.shape[2]
    model = x.shape[1]
    mine = left.shape[1]
    _, three, cols = p.shape
    width = three // 3
    def load(src, dst, n):
        return pltpu.make_async_copy(src, dst, in_sem.at[n])

    lefts = load(left_a, left.at[:, :, pl.ds(0, rows)], 0)
    theirs = [load(packed_b.at[:, pl.ds(2 * model + m * mine, mine)], acts.at[m], 1 + m) for m in range(3)]
    sides = []
    for j, side in enumerate((x, g)):
        for i, src in enumerate((packed_a, packed_b)):
            sides.append(load(src.at[:, pl.ds(j * model, model)], side.at[pl.ds(i * rows, rows)], 4 + 2 * j + i))
    for copy in theirs + [lefts] + sides:
        copy.start()
    for m in range(3):
        theirs[m].wait()
        left[m, :, rows:] = acts[m].T
    lefts.wait()
    outs = []
    dsts = (d0, d1, d2, d3)
    for m, right in enumerate((x, x, g)):
        for copy in (sides[0:2], [], sides[2:4])[m]:
            copy.wait()
        for i, (half, pair) in enumerate(jobs):
            lhs = jnp.concatenate([left[m, k * width : (k + 1) * width, :] for k in pair], axis=0)
            found = nn(lhs, right[:, half * cols : (half + 1) * cols]).astype(BF)
            for j in range(2):
                p[2 * i + j, m * width : (m + 1) * width, :] = found[j * width : (j + 1) * width]
                at = pl.ds(m * width, width)
                copy = pltpu.make_async_copy(p.at[2 * i + j, at], dsts[2 * i + j].at[at], out_sem.at[m, 2 * i + j])
                copy.start()
                outs.append(copy)
    for copy in outs:
        copy.wait()


def sums_call(packed, left, theirs, pieces, jobs, name):
    _, mine, rows = left.shape
    width = (packed.shape[1] - 3 * mine) // 2
    three = 3 * mine // pieces
    hbm = pl.BlockSpec(memory_space=pl.ANY)
    return pl.pallas_call(
        functools.partial(sums_kernel, jobs),
        in_specs=[hbm] * 3,
        out_specs=[hbm] * 4,
        out_shape=(jax.ShapeDtypeStruct((three, width // 2), BF),) * 4,
        scratch_shapes=[
            pltpu.VMEM((2 * rows, width), BF),
            pltpu.VMEM((2 * rows, width), BF),
            pltpu.VMEM((3, mine, 2 * rows), BF),
            pltpu.VMEM((3, rows, mine), BF),
            pltpu.VMEM((4, three, width // 2), BF),
            pltpu.SemaphoreType.DMA((8,)),
            pltpu.SemaphoreType.DMA((3, 4)),
        ],
        compiler_params=pltpu.CompilerParams(vmem_limit_bytes=SUMS_LIMIT),
        cost_estimate=pl.CostEstimate(flops=6 * rows * mine * width, bytes_accessed=16 * rows * width, transcendentals=0),
        name=name,
    )(packed, left, theirs)


def grads_kernel(q0a, q0b, q1a, q1b, q2a, q2b, o_gate, o_up, o_down, q, total, q_sem, o_sem):
    cols = q.shape[2] // 2
    loads = [
        pltpu.make_async_copy(src, q.at[k // 2, :, pl.ds((k % 2) * cols, cols)], q_sem.at[k]) for k, src in enumerate((q0a, q0b, q1a, q1b, q2a, q2b))
    ]
    for copy in loads:
        copy.start()
    for copy in loads:
        copy.wait()
    stores = []
    width = total.shape[1]
    for m, dst in enumerate((o_gate, o_up, o_down)):
        at = slice(m * width, (m + 1) * width)
        terms = [q[k, at].astype(F32) for k in range(3)]
        total[m] = terms[0] + terms[1] + terms[2]
        copy = pltpu.make_async_copy(total.at[m], dst.at[0], o_sem.at[m])
        copy.start()
        stores.append(copy)
    for copy in stores:
        copy.wait()


def after_kernel(capacity, table, scaled_in, notes, pool, norm, gain, out, grad, out_buf, grad_buf, sem):
    rows, model = scaled_in.shape
    factor = out.shape[0] // rows
    inv, gate0, gate1 = notes[:, 0:1], notes[:, 3:4], notes[:, 4:5]
    slot0, slot1 = notes[:, 1:2].astype(jnp.int32), notes[:, 2:3].astype(jnp.int32)
    place = iota((rows, table.shape[0]), 1)
    grad0, grad1 = slot0 + capacity, slot1 + capacity
    sel = jnp.concatenate(
        [
            jnp.where(place == slot0, 1.0, 0.0).astype(BF),
            jnp.where(place == slot1, 1.0, 0.0).astype(BF),
            jnp.where((place == grad0) | (place == grad1), 1.0, 0.0).astype(BF),
        ],
        axis=0,
    )
    band = rows // 3
    mix = jnp.concatenate([pick(band, factor, j) for j in range(factor)], axis=0)
    copies = []

    def store(values, scale, buf, dst, first):
        for i in range(3):
            part = values[i * band : (i + 1) * band]
            blocks = jnp.concatenate([(scale[j : j + 1, :] * part).astype(BF) for j in range(factor)], axis=0)
            at = slice(i * band * factor, (i + 1) * band * factor)
            buf[at, :] = tn(mix, blocks).astype(BF)
            span = pl.ds(i * band * factor, band * factor)
            copy = pltpu.make_async_copy(buf.at[span], dst.at[span], sem.at[first + i])
            copy.start()
            copies.append(copy)

    found = nn(sel, table[...])
    mixture = gate0 * found[:rows] + gate1 * found[rows : 2 * rows]
    store(mixture, gain, out_buf, out, 0)
    d_scaled = found[2 * rows :] * norm[...]
    scaled = scaled_in[...]
    d_short = inv * (d_scaled - scaled * jnp.mean(d_scaled * scaled, axis=1, keepdims=True))
    store(d_short, pool, grad_buf, grad, 3)
    for copy in copies:
        copy.wait()


def shards(
    tokens,
    cotangent,
    expert_ids,
    votes,
    pool_weight,
    norm_gain,
    up_gain,
    gate_weight,
    up_weight,
    down_weight,
):
    ring = lax.axis_size("y")
    experts = lax.axis_size("z") * lax.axis_size("x")
    rows, top = expert_ids.shape
    width = tokens.shape[1]
    hidden = gate_weight.shape[1]
    capacity = 2 * rows * top // experts
    slots = 2 * experts * capacity
    params = pltpu.CompilerParams(vmem_limit_bytes=EDGE_LIMIT)
    vmem = pl.BlockSpec(memory_space=pltpu.VMEM)
    hbm = pl.BlockSpec(memory_space=pl.ANY)
    norm = norm_gain[None]
    ids, counts = expert_ids.T, votes.T

    def move(a, k):
        return lax.ppermute(a, "y", [(i, (i + k) % ring) for i in range(ring)])

    def swap(a):
        return lax.ppermute(a, "core", [(0, 1), (1, 0)])

    def exchange(a):
        return lax.all_to_all(a, ("z", "x"), split_axis=0, concat_axis=0, tiled=True)

    up, down = 1, ring - 1
    h0, h1 = pl.pallas_call(
        pack_kernel,
        in_specs=[hbm] * 3,
        out_specs=[hbm] * 2,
        out_shape=(jax.ShapeDtypeStruct((3 * hidden // 2, width), BF),) * 2,
        scratch_shapes=[pltpu.VMEM((3 * hidden, width), BF), pltpu.SemaphoreType.DMA((3,)), pltpu.SemaphoreType.DMA((2,))],
        compiler_params=params,
        name="pack",
    )(gate_weight, up_weight, down_weight)
    u0, d1 = move(h0, up), move(h1, down)
    t0, t1 = move(u0, up), move(d1, down)
    u1, d0 = move(h1, up), move(h0, down)
    halves = [h0, h1, u0, u1, t0, t1, d0, d1]
    least = jnp.asarray(jnp.finfo(BF).min, BF)
    halves = [jnp.maximum(h0, least), jnp.maximum(h1, least), *halves[2:]] + [swap(a) for a in halves]

    send, scaled, notes = pl.pallas_call(
        functools.partial(before_kernel, experts, capacity),
        out_shape=(
            jax.ShapeDtypeStruct((slots, width), BF),
            jax.ShapeDtypeStruct((rows, width), F32),
            jax.ShapeDtypeStruct((rows, 128), F32),
        ),
        compiler_params=params,
        name="before",
    )(tokens, cotangent, ids, counts, pool_weight, norm, up_gain)

    arrived = exchange(send)
    back, packed, left = experts_call(arrived, halves, capacity)
    theirs = swap(packed)
    returned = exchange(back)
    p2a, p3a, p1b, p2b = sums_call(packed, left, theirs, ring, ((0, (2, 3)), (1, (1, 2))), "sums_far")
    p0a, p1a, p3b, p0b = sums_call(packed, left, theirs, ring, ((0, (0, 1)), (1, (3, 0))), "sums_near")
    r1b, r3a = move(p1b, down), move(p3a, up)
    r1a = move(p1a + move(p2a, down), down)
    r3b = move(p3b + move(p2b, up), up)
    parts = (p0a, p0b, r1a, r1b, r3a, r3b)

    held = jax.ShapeDtypeStruct((1, hidden, width), F32)
    grads = pl.pallas_call(
        grads_kernel,
        in_specs=[hbm] * 6,
        out_specs=[hbm] * 3,
        out_shape=(held, held, held),
        scratch_shapes=[
            pltpu.VMEM((3, 3 * hidden, width), BF),
            pltpu.VMEM((3, hidden, width), F32),
            pltpu.SemaphoreType.DMA((6,)),
            pltpu.SemaphoreType.DMA((3,)),
        ],
        compiler_params=params,
        name="grads",
    )(*parts)

    shape = jax.ShapeDtypeStruct(tokens.shape, BF)
    layer_out, tokens_grad = pl.pallas_call(
        functools.partial(after_kernel, capacity),
        in_specs=[vmem] * 6,
        out_specs=[hbm] * 2,
        out_shape=(shape, shape),
        scratch_shapes=[pltpu.VMEM(tokens.shape, BF), pltpu.VMEM(tokens.shape, BF), pltpu.SemaphoreType.DMA((6,))],
        compiler_params=pltpu.CompilerParams(vmem_limit_bytes=AFTER_LIMIT),
        name="after",
    )(returned, scaled, notes, pool_weight, norm, up_gain)
    return (layer_out, tokens_grad, *grads)


def solution(mesh):
    sizes = (mesh.shape["dp"] // 2, 2, mesh.shape["expert"] // 4, 4)
    mesh = jax.sharding.Mesh(mesh.devices.reshape(sizes), ("y", "core", "z", "x"))
    rows = P(("y", "core", "z", "x"), None)
    held = P(("z", "x"), ("y", "core"), None)
    return jax.shard_map(
        shards,
        mesh=mesh,
        in_specs=(rows, rows, rows, rows, P(), P(), P(), held, held, held),
        out_specs=(rows, rows, held, held, held),
        check_vma=False,
    )
```

profile of v0, /device:TPU:26, one launch (start us, length us, event | category | flops | bytes accessed | tf_op | source)
XLA Modules:
  0.0 190.6 jit_solution(17146755462565499896)
XLA Ops:
  0.6 6.2 %before.1 = (bf16[768,2048]{1,0:T(8,128)(2,1)}, f32[96,2048]{1,0:T(8,128)}, f32[96,128]{1,0:T(8,128)}) custom-call(bf16[288,2048]{1,0:T(8,128)(2,1)} %tokens.1, bf16[288,2048]{1,0:T(8,128)(2,1)} %cotangent.1, s32[2,96]{1,0:T(2,128)} %bitcast.11, s32[2,96]{1,0:T(2,128)} %bitcast.12, f32[3,2048]{1,0:T(4,128)} %pool.3, f32[1,2048]{1,0:T(1,128)} %bitcast.7, ...), custom_call_target="tpu_custom_call" | custom-call | tf_op jit(solution)/shard_map/before/pallas_call | solution.py:424
  6.8 11.7 %all-to-all-start = ((bf16[32,24,2048]{2,1,0:T(8,128)(2,1)}), bf16[32,24,2048]{2,1,0:T(8,128)(2,1)}, u32[]{:S(2)}, u32[]{:S(2)}) async-start(bf16[32,24,2048]{2,1,0:T(8,128)(2,1)} %bitcast.9), calls=%async_computation | async-start | bytes 6291456 | tf_op jit(solution)/shard_map/all_to_all | solution.py:405
  18.5 2.4 %pack.1 = (bf16[192,2048]{1,0:T(8,128)(2,1)}, bf16[192,2048]{1,0:T(8,128)(2,1)}) custom-call(bf16[1,128,2048]{2,1,0:T(8,128)(2,1)} %w_gate.1, bf16[1,128,2048]{2,1,0:T(8,128)(2,1)} %w_up.1, bf16[1,128,2048]{2,1,0:T(8,128)(2,1)} %w_down.1), custom_call_target="tpu_custom_call" | custom-call | tf_op jit(solution)/shard_map/pack/pallas_call | solution.py:408
  21.8 2.5 %collective-permute-start = (bf16[192,2048]{1,0:T(8,128)(2,1)}, bf16[192,2048]{1,0:T(8,128)(2,1)S(1)}, u32[]{:S(2)}, u32[]{:S(2)}) collective-permute-start(bf16[192,2048]{1,0:T(8,128)(2,1)} %get-tuple-element.27), channel_id=1, source_target_pairs={{0,64},{64,128},{128,192},{192,0},{1,65},{65,129},{129,193},{193,1... | collective-permute-start | bytes 2359304 | tf_op jit(solution)/shard_map/ppermute | solution.py:399
  24.3 3.3 %collective-permute-start.1 = (bf16[192,2048]{1,0:T(8,128)(2,1)}, bf16[192,2048]{1,0:T(8,128)(2,1)S(1)}, u32[]{:S(2)}, u32[]{:S(2)}) collective-permute-start(bf16[192,2048]{1,0:T(8,128)(2,1)} %get-tuple-element.28), channel_id=1, source_target_pairs={{0,64},{64,128},{128,192},{192,0},{1,65},{65,129},{129,193},{193,1... | collective-permute-start | bytes 2359304 | tf_op jit(solution)/shard_map/ppermute | solution.py:399
  27.6 15.2 %collective-permute-done.5.refs_6_ = bf16[192,2048]{1,0:T(8,128)(2,1)S(1)} collective-permute-done((bf16[192,2048]{1,0:T(8,128)(2,1)}, bf16[192,2048]{1,0:T(8,128)(2,1)S(1)}, u32[]{:S(2)}, u32[]{:S(2)}) %collective-permute-start.5) | collective-permute-done | bytes 786464 | tf_op jit(solution)/shard_map/ppermute | solution.py:399
  42.8 3.3 %collective-permute-start.2 = (bf16[192,2048]{1,0:T(8,128)(2,1)S(1)}, bf16[192,2048]{1,0:T(8,128)(2,1)S(1)}, u32[]{:S(2)}, u32[]{:S(2)}) collective-permute-start(bf16[192,2048]{1,0:T(8,128)(2,1)S(1)} %collective-permute-done.refs_2_), channel_id=1, source_target_pairs={{0,64},{64,128},{128,192},{192,0},{1,65},{65,129},{129,193},{193,1... | collective-permute-start | bytes 2359304 | tf_op jit(solution)/shard_map/ppermute | solution.py:399
  46.1 13.1 %collective-permute-done.3.refs_7_ = bf16[192,2048]{1,0:T(8,128)(2,1)S(1)} collective-permute-done((bf16[192,2048]{1,0:T(8,128)(2,1)}, bf16[192,2048]{1,0:T(8,128)(2,1)S(1)}, u32[]{:S(2)}, u32[]{:S(2)}) %collective-permute-start.3) | collective-permute-done | bytes 786464 | tf_op jit(solution)/shard_map/ppermute | solution.py:399
  59.9 15.4 %collective-permute-done.2.refs_4_ = bf16[192,2048]{1,0:T(8,128)(2,1)S(1)} collective-permute-done((bf16[192,2048]{1,0:T(8,128)(2,1)S(1)}, bf16[192,2048]{1,0:T(8,128)(2,1)S(1)}, u32[]{:S(2)}, u32[]{:S(2)}) %collective-permute-start.2) | collective-permute-done | bytes 786464 | tf_op jit(solution)/shard_map/ppermute | solution.py:399
  75.3 4.3 %collective-permute-done.4.refs_5_ = bf16[192,2048]{1,0:T(8,128)(2,1)S(1)} collective-permute-done((bf16[192,2048]{1,0:T(8,128)(2,1)S(1)}, bf16[192,2048]{1,0:T(8,128)(2,1)S(1)}, u32[]{:S(2)}, u32[]{:S(2)}) %collective-permute-start.4) | collective-permute-done | bytes 786464 | tf_op jit(solution)/shard_map/ppermute | solution.py:399
  83.7 6.0 %all-to-all-done = bf16[32,24,2048]{2,1,0:T(8,128)(2,1)} async-done(((bf16[32,24,2048]{2,1,0:T(8,128)(2,1)}), bf16[32,24,2048]{2,1,0:T(8,128)(2,1)}, u32[]{:S(2)}, u32[]{:S(2)}) %all-to-all-start) | async-done | bytes 3145760 | tf_op jit(solution)/shard_map/all_to_all | solution.py:405
  89.8 16.2 %experts.1 = (bf16[768,2048]{1,0:T(8,128)(2,1)}, bf16[384,5632]{1,0:T(8,128)(2,1)}, bf16[3,512,384]{2,1,0:T(8,128)(2,1)}) custom-call(bf16[768,2048]{1,0:T(8,128)(2,1)} %bitcast.4.arrived, bf16[192,2048]{1,0:T(8,128)(2,1)S(1)} %get-tuple-element.48.refs_0_, bf16[192,2048]{1,0:T(8,128)(2,1)S(1)} %get-tuple-element.47.refs_1_, ...), custom_call_target="tpu_custom_call" | custom-call | flops 9663676416 | bytes 12582912 | tf_op jit(solution)/shard_map/experts/pallas_call | solution.py:219
  106.0 7.4 %all-to-all-start.1 = ((bf16[32,24,2048]{2,1,0:T(8,128)(2,1)}), bf16[32,24,2048]{2,1,0:T(8,128)(2,1)}, u32[]{:S(2)}, u32[]{:S(2)}) async-start(bf16[32,24,2048]{2,1,0:T(8,128)(2,1)} %bitcast.10), calls=%async_computation.1 | async-start | bytes 6291456 | tf_op jit(solution)/shard_map/all_to_all | solution.py:405
  113.7 6.4 %sums_far.1 = (bf16[384,1024]{1,0:T(8,128)(2,1)}, bf16[384,1024]{1,0:T(8,128)(2,1)}, bf16[384,1024]{1,0:T(8,128)(2,1)}, bf16[384,1024]{1,0:T(8,128)(2,1)}) custom-call(bf16[384,5632]{1,0:T(8,128)(2,1)} %get-tuple-element.34.packed_a, bf16[3,512,384]{2,1,0:T(8,128)(2,1)} %get-tuple-element.35.left_a, bf16[384,5632]{1,0:T(8,128)(2,1)} %collective-permute-done.14.packed_b), custom_call_target="tpu_custom_call" | custom-call | flops 2415919104 | bytes 12582912 | tf_op jit(solution)/shard_map/sums_far/pallas_call | solution.py:290
  120.9 2.5 %collective-permute-start.19 = (bf16[384,1024]{1,0:T(8,128)(2,1)}, bf16[384,1024]{1,0:T(8,128)(2,1)S(1)}, u32[]{:S(2)}, u32[]{:S(2)}) collective-permute-start(bf16[384,1024]{1,0:T(8,128)(2,1)} %get-tuple-element.43), channel_id=1, source_target_pairs={{0,64},{64,128},{128,192},{192,0},{1,65},{65,129},{129,193},{193,1... | collective-permute-start | bytes 2359304 | tf_op jit(solution)/shard_map/ppermute | solution.py:399
  123.4 3.2 %collective-permute-start.18 = (bf16[384,1024]{1,0:T(8,128)(2,1)}, bf16[384,1024]{1,0:T(8,128)(2,1)S(1)}, u32[]{:S(2)}, u32[]{:S(2)}) collective-permute-start(bf16[384,1024]{1,0:T(8,128)(2,1)} %get-tuple-element.41), channel_id=1, source_target_pairs={{0,64},{64,128},{128,192},{192,0},{1,65},{65,129},{129,193},{193,1... | collective-permute-start | bytes 2359304 | tf_op jit(solution)/shard_map/ppermute | solution.py:399
  126.6 6.3 %sums_near.1 = (bf16[384,1024]{1,0:T(8,128)(2,1)}, bf16[384,1024]{1,0:T(8,128)(2,1)}, bf16[384,1024]{1,0:T(8,128)(2,1)}, bf16[384,1024]{1,0:T(8,128)(2,1)}) custom-call(bf16[384,5632]{1,0:T(8,128)(2,1)} %get-tuple-element.34.packed_a, bf16[3,512,384]{2,1,0:T(8,128)(2,1)} %get-tuple-element.35.left_a, bf16[384,5632]{1,0:T(8,128)(2,1)} %collective-permute-done.14.packed_b), custom_call_target="tpu_custom_call" | custom-call | flops 2415919104 | bytes 12582912 | tf_op jit(solution)/shard_map/sums_near/pallas_call | solution.py:290
  133.0 9.0 %collective-permute-done.15 = bf16[384,1024]{1,0:T(8,128)(2,1)S(1)} collective-permute-done((bf16[384,1024]{1,0:T(8,128)(2,1)}, bf16[384,1024]{1,0:T(8,128)(2,1)S(1)}, u32[]{:S(2)}, u32[]{:S(2)}) %collective-permute-start.15) | collective-permute-done | bytes 786464 | tf_op jit(solution)/shard_map/ppermute | solution.py:399
  145.1 3.3 %collective-permute-start.20 = (bf16[384,1024]{1,0:T(8,128)(2,1)S(1)}, bf16[384,1024]{1,0:T(8,128)(2,1)}, u32[]{:S(2)}, u32[]{:S(2)}) collective-permute-start(bf16[384,1024]{1,0:T(8,128)(2,1)S(1)} %add.7), channel_id=1, source_target_pairs={{0,64},{64,128},{128,192},{192,0},{1,65},{65,129},{129,193},{193,1... | collective-permute-start | bytes 2359304 | tf_op jit(solution)/shard_map/ppermute | solution.py:399
  148.3 10.5 %collective-permute-done.17.q1b = bf16[384,1024]{1,0:T(8,128)(2,1)S(1)} collective-permute-done((bf16[384,1024]{1,0:T(8,128)(2,1)}, bf16[384,1024]{1,0:T(8,128)(2,1)S(1)}, u32[]{:S(2)}, u32[]{:S(2)}) %collective-permute-start.17) | collective-permute-done | bytes 786464 | tf_op jit(solution)/shard_map/ppermute | solution.py:399
  158.8 16.0 %collective-permute-done.16.q1a = bf16[384,1024]{1,0:T(8,128)(2,1)S(1)} collective-permute-done((bf16[384,1024]{1,0:T(8,128)(2,1)S(1)}, bf16[384,1024]{1,0:T(8,128)(2,1)S(1)}, u32[]{:S(2)}, u32[]{:S(2)}) %collective-permute-start.16) | collective-permute-done | bytes 786464 | tf_op jit(solution)/shard_map/ppermute | solution.py:399
  175.7 4.2 %grads.1 = (f32[1,128,2048]{2,1,0:T(8,128)}, f32[1,128,2048]{2,1,0:T(8,128)}, f32[1,128,2048]{2,1,0:T(8,128)}) custom-call(bf16[384,1024]{1,0:T(8,128)(2,1)} %get-tuple-element.36.q0a, bf16[384,1024]{1,0:T(8,128)(2,1)} %get-tuple-element.37.q0b, bf16[384,1024]{1,0:T(8,128)(2,1)} %copy-done.7, bf16[384,1024]{1,0:T(8,128)(2,1)} %copy-done.5, ...), custom_call_target="tpu_custom_call" | custom-call | tf_op jit(solution)/shard_map/grads/pallas_call | solution.py:447
  180.0 5.8 %all-to-all-done.1 = bf16[32,24,2048]{2,1,0:T(8,128)(2,1)} async-done(((bf16[32,24,2048]{2,1,0:T(8,128)(2,1)}), bf16[32,24,2048]{2,1,0:T(8,128)(2,1)}, u32[]{:S(2)}, u32[]{:S(2)}) %all-to-all-start.1) | async-done | bytes 3145760 | tf_op jit(solution)/shard_map/all_to_all | solution.py:405
  185.8 4.7 %after.1 = (bf16[288,2048]{1,0:T(8,128)(2,1)}, bf16[288,2048]{1,0:T(8,128)(2,1)}) custom-call(bf16[768,2048]{1,0:T(8,128)(2,1)} %bitcast.6.table, f32[96,2048]{1,0:T(8,128)S(1)} %copy-done, f32[96,128]{1,0:T(8,128)S(1)} %copy-done.3, f32[3,2048]{1,0:T(4,128)S(1)} %copy-done.1, f32[1,2048]{1,0:T(1,128)S(1)} %bitcast.8, f32[3,2048]{1,0:T(4,128)S(1)} %copy-done.2), custom_call_target="tpu_custom_call" | custom-call | tf_op jit(solution)/shard_map/after/pallas_call | solution.py:463
  (72 shorter events, 10.8 us)
Async XLA Ops:
  6.8 83.0 %all-to-all-start = ((bf16[32,24,2048]{2,1,0:T(8,128)(2,1)}), bf16[32,24,2048]{2,1,0:T(8,128)(2,1)}, u32[]{:S(2)}, u32[]{:S(2)}) async-start(bf16[32,24,2048]{2,1,0:T(8,128)(2,1)} %bitcast.9), calls=%async_computation | async-start | bytes 6291456 | tf_op jit(solution)/shard_map/all_to_all | solution.py:405
  20.9 3.4 %collective-permute-start.6 = (bf16[192,2048]{1,0:T(8,128)(2,1)}, bf16[192,2048]{1,0:T(8,128)(2,1)S(1)}, u32[]{:S(2)}, u32[]{:S(2)}) collective-permute-start(bf16[192,2048]{1,0:T(8,128)(2,1)} %get-tuple-element.27), channel_id=1, source_target_pairs={{0,32},{32,0},{1,33},{33,1},{2,34},{34,2},{3,35},{35,3},{4,36},{36... | collective-permute-start | bytes 2359304 | tf_op jit(solution)/shard_map/ppermute | solution.py:402
  20.9 21.8 %collective-permute-start.5 = (bf16[192,2048]{1,0:T(8,128)(2,1)}, bf16[192,2048]{1,0:T(8,128)(2,1)S(1)}, u32[]{:S(2)}, u32[]{:S(2)}) collective-permute-start(bf16[192,2048]{1,0:T(8,128)(2,1)} %get-tuple-element.27), channel_id=1, source_target_pairs={{0,192},{64,0},{128,64},{192,128},{1,193},{65,1},{129,65},{193,129... | collective-permute-start | bytes 2359304 | tf_op jit(solution)/shard_map/ppermute | solution.py:399
  21.8 21.0 %collective-permute-start = (bf16[192,2048]{1,0:T(8,128)(2,1)}, bf16[192,2048]{1,0:T(8,128)(2,1)S(1)}, u32[]{:S(2)}, u32[]{:S(2)}) collective-permute-start(bf16[192,2048]{1,0:T(8,128)(2,1)} %get-tuple-element.27), channel_id=1, source_target_pairs={{0,64},{64,128},{128,192},{192,0},{1,65},{65,129},{129,193},{193,1... | collective-permute-start | bytes 2359304 | tf_op jit(solution)/shard_map/ppermute | solution.py:399
  24.3 34.9 %collective-permute-start.3 = (bf16[192,2048]{1,0:T(8,128)(2,1)}, bf16[192,2048]{1,0:T(8,128)(2,1)S(1)}, u32[]{:S(2)}, u32[]{:S(2)}) collective-permute-start(bf16[192,2048]{1,0:T(8,128)(2,1)} %get-tuple-element.28), channel_id=1, source_target_pairs={{0,192},{64,0},{128,64},{192,128},{1,193},{65,1},{129,65},{193,129... | collective-permute-start | bytes 2359304 | tf_op jit(solution)/shard_map/ppermute | solution.py:399
  24.3 34.9 %collective-permute-start.7 = (bf16[192,2048]{1,0:T(8,128)(2,1)}, bf16[192,2048]{1,0:T(8,128)(2,1)S(1)}, u32[]{:S(2)}, u32[]{:S(2)}) collective-permute-start(bf16[192,2048]{1,0:T(8,128)(2,1)} %get-tuple-element.28), channel_id=1, source_target_pairs={{0,32},{32,0},{1,33},{33,1},{2,34},{34,2},{3,35},{35,3},{4,36},{36... | collective-permute-start | bytes 2359304 | tf_op jit(solution)/shard_map/ppermute | solution.py:402
  24.3 65.5 %copy-start.8 = (bf16[192,2048]{1,0:T(8,128)(2,1)}, bf16[192,2048]{1,0:T(8,128)(2,1)S(1)}, u32[]{:S(2)}) copy-start(bf16[192,2048]{1,0:T(8,128)(2,1)S(1)} %collective-permute-done.6.refs_8_) | copy-start | bytes 2359300
  24.3 35.1 %collective-permute-start.1 = (bf16[192,2048]{1,0:T(8,128)(2,1)}, bf16[192,2048]{1,0:T(8,128)(2,1)S(1)}, u32[]{:S(2)}, u32[]{:S(2)}) collective-permute-start(bf16[192,2048]{1,0:T(8,128)(2,1)} %get-tuple-element.28), channel_id=1, source_target_pairs={{0,64},{64,128},{128,192},{192,0},{1,65},{65,129},{129,193},{193,1... | collective-permute-start | bytes 2359304 | tf_op jit(solution)/shard_map/ppermute | solution.py:399
  42.8 17.0 %collective-permute-start.12 = (bf16[192,2048]{1,0:T(8,128)(2,1)S(1)}, bf16[192,2048]{1,0:T(8,128)(2,1)S(1)}, u32[]{:S(2)}, u32[]{:S(2)}) collective-permute-start(bf16[192,2048]{1,0:T(8,128)(2,1)S(1)} %collective-permute-done.5.refs_6_), channel_id=1, source_target_pairs={{0,32},{32,0},{1,33},{33,1},{2,34},{34,2},{3,35},{35,3},{4,36},{36... | collective-permute-start | bytes 2359304 | tf_op jit(solution)/shard_map/ppermute | solution.py:402
  42.8 32.5 %collective-permute-start.2 = (bf16[192,2048]{1,0:T(8,128)(2,1)S(1)}, bf16[192,2048]{1,0:T(8,128)(2,1)S(1)}, u32[]{:S(2)}, u32[]{:S(2)}) collective-permute-start(bf16[192,2048]{1,0:T(8,128)(2,1)S(1)} %collective-permute-done.refs_2_), channel_id=1, source_target_pairs={{0,64},{64,128},{128,192},{192,0},{1,65},{65,129},{129,193},{193,1... | collective-permute-start | bytes 2359304 | tf_op jit(solution)/shard_map/ppermute | solution.py:399
  59.2 20.4 %collective-permute-start.4 = (bf16[192,2048]{1,0:T(8,128)(2,1)S(1)}, bf16[192,2048]{1,0:T(8,128)(2,1)S(1)}, u32[]{:S(2)}, u32[]{:S(2)}) collective-permute-start(bf16[192,2048]{1,0:T(8,128)(2,1)S(1)} %collective-permute-done.3.refs_7_), channel_id=1, source_target_pairs={{0,192},{64,0},{128,64},{192,128},{1,193},{65,1},{129,65},{193,129... | collective-permute-start | bytes 2359304 | tf_op jit(solution)/shard_map/ppermute | solution.py:399
  59.2 22.2 %collective-permute-start.8 = (bf16[192,2048]{1,0:T(8,128)(2,1)S(1)}, bf16[192,2048]{1,0:T(8,128)(2,1)S(1)}, u32[]{:S(2)}, u32[]{:S(2)}) collective-permute-start(bf16[192,2048]{1,0:T(8,128)(2,1)S(1)} %collective-permute-done.refs_2_), channel_id=1, source_target_pairs={{0,32},{32,0},{1,33},{33,1},{2,34},{34,2},{3,35},{35,3},{4,36},{36... | collective-permute-start | bytes 2359304 | tf_op jit(solution)/shard_map/ppermute | solution.py:402
  59.3 22.1 %collective-permute-start.13 = (bf16[192,2048]{1,0:T(8,128)(2,1)S(1)}, bf16[192,2048]{1,0:T(8,128)(2,1)S(1)}, u32[]{:S(2)}, u32[]{:S(2)}) collective-permute-start(bf16[192,2048]{1,0:T(8,128)(2,1)S(1)} %collective-permute-done.3.refs_7_), channel_id=1, source_target_pairs={{0,32},{32,0},{1,33},{33,1},{2,34},{34,2},{3,35},{35,3},{4,36},{36... | collective-permute-start | bytes 2359304 | tf_op jit(solution)/shard_map/ppermute | solution.py:402
  59.8 21.7 %collective-permute-start.9 = (bf16[192,2048]{1,0:T(8,128)(2,1)S(1)}, bf16[192,2048]{1,0:T(8,128)(2,1)S(1)}, u32[]{:S(2)}, u32[]{:S(2)}) collective-permute-start(bf16[192,2048]{1,0:T(8,128)(2,1)S(1)} %collective-permute-done.1.refs_3_), channel_id=1, source_target_pairs={{0,32},{32,0},{1,33},{33,1},{2,34},{34,2},{3,35},{35,3},{4,36},{36... | collective-permute-start | bytes 2359304 | tf_op jit(solution)/shard_map/ppermute | solution.py:402
  75.3 6.2 %collective-permute-start.10 = (bf16[192,2048]{1,0:T(8,128)(2,1)S(1)}, bf16[192,2048]{1,0:T(8,128)(2,1)S(1)}, u32[]{:S(2)}, u32[]{:S(2)}) collective-permute-start(bf16[192,2048]{1,0:T(8,128)(2,1)S(1)} %collective-permute-done.2.refs_4_), channel_id=1, source_target_pairs={{0,32},{32,0},{1,33},{33,1},{2,34},{34,2},{3,35},{35,3},{4,36},{36... | collective-permute-start | bytes 2359304 | tf_op jit(solution)/shard_map/ppermute | solution.py:402
  79.6 4.1 %collective-permute-start.11 = (bf16[192,2048]{1,0:T(8,128)(2,1)S(1)}, bf16[192,2048]{1,0:T(8,128)(2,1)}, u32[]{:S(2)}, u32[]{:S(2)}) collective-permute-start(bf16[192,2048]{1,0:T(8,128)(2,1)S(1)} %collective-permute-done.4.refs_5_), channel_id=1, source_target_pairs={{0,32},{32,0},{1,33},{33,1},{2,34},{34,2},{3,35},{35,3},{4,36},{36... | collective-permute-start | bytes 2359304 | tf_op jit(solution)/shard_map/ppermute | solution.py:402
  105.9 7.8 %collective-permute-start.14 = (bf16[384,5632]{1,0:T(8,128)(2,1)}, bf16[384,5632]{1,0:T(8,128)(2,1)}, u32[]{:S(2)}, u32[]{:S(2)}) collective-permute-start(bf16[384,5632]{1,0:T(8,128)(2,1)} %get-tuple-element.34.packed_a), channel_id=1, source_target_pairs={{0,32},{32,0},{1,33},{33,1},{2,34},{34,2},{3,35},{35,3},{4,36},{36... | collective-permute-start | bytes 12976136 | tf_op jit(solution)/shard_map/ppermute | solution.py:402
  106.0 79.7 %all-to-all-start.1 = ((bf16[32,24,2048]{2,1,0:T(8,128)(2,1)}), bf16[32,24,2048]{2,1,0:T(8,128)(2,1)}, u32[]{:S(2)}, u32[]{:S(2)}) async-start(bf16[32,24,2048]{2,1,0:T(8,128)(2,1)} %bitcast.10), calls=%async_computation.1 | async-start | bytes 6291456 | tf_op jit(solution)/shard_map/all_to_all | solution.py:405
  120.1 21.9 %collective-permute-start.15 = (bf16[384,1024]{1,0:T(8,128)(2,1)}, bf16[384,1024]{1,0:T(8,128)(2,1)S(1)}, u32[]{:S(2)}, u32[]{:S(2)}) collective-permute-start(bf16[384,1024]{1,0:T(8,128)(2,1)} %get-tuple-element.39), channel_id=1, source_target_pairs={{0,192},{64,0},{128,64},{192,128},{1,193},{65,1},{129,65},{193,129... | collective-permute-start | bytes 2359304 | tf_op jit(solution)/shard_map/ppermute | solution.py:399
  120.9 22.6 %collective-permute-start.19 = (bf16[384,1024]{1,0:T(8,128)(2,1)}, bf16[384,1024]{1,0:T(8,128)(2,1)S(1)}, u32[]{:S(2)}, u32[]{:S(2)}) collective-permute-start(bf16[384,1024]{1,0:T(8,128)(2,1)} %get-tuple-element.43), channel_id=1, source_target_pairs={{0,64},{64,128},{128,192},{192,0},{1,65},{65,129},{129,193},{193,1... | collective-permute-start | bytes 2359304 | tf_op jit(solution)/shard_map/ppermute | solution.py:399
  123.4 35.4 %collective-permute-start.17 = (bf16[384,1024]{1,0:T(8,128)(2,1)}, bf16[384,1024]{1,0:T(8,128)(2,1)S(1)}, u32[]{:S(2)}, u32[]{:S(2)}) collective-permute-start(bf16[384,1024]{1,0:T(8,128)(2,1)} %get-tuple-element.40), channel_id=1, source_target_pairs={{0,192},{64,0},{128,64},{192,128},{1,193},{65,1},{129,65},{193,129... | collective-permute-start | bytes 2359304 | tf_op jit(solution)/shard_map/ppermute | solution.py:399
  123.4 35.4 %collective-permute-start.18 = (bf16[384,1024]{1,0:T(8,128)(2,1)}, bf16[384,1024]{1,0:T(8,128)(2,1)S(1)}, u32[]{:S(2)}, u32[]{:S(2)}) collective-permute-start(bf16[384,1024]{1,0:T(8,128)(2,1)} %get-tuple-element.41), channel_id=1, source_target_pairs={{0,64},{64,128},{128,192},{192,0},{1,65},{65,129},{129,193},{193,1... | collective-permute-start | bytes 2359304 | tf_op jit(solution)/shard_map/ppermute | solution.py:399
  143.4 31.5 %collective-permute-start.16 = (bf16[384,1024]{1,0:T(8,128)(2,1)S(1)}, bf16[384,1024]{1,0:T(8,128)(2,1)S(1)}, u32[]{:S(2)}, u32[]{:S(2)}) collective-permute-start(bf16[384,1024]{1,0:T(8,128)(2,1)S(1)} %add.6), channel_id=1, source_target_pairs={{0,192},{64,0},{128,64},{192,128},{1,193},{65,1},{129,65},{193,129... | collective-permute-start | bytes 2359304 | tf_op jit(solution)/shard_map/ppermute | solution.py:399
  145.1 29.8 %collective-permute-start.20 = (bf16[384,1024]{1,0:T(8,128)(2,1)S(1)}, bf16[384,1024]{1,0:T(8,128)(2,1)}, u32[]{:S(2)}, u32[]{:S(2)}) collective-permute-start(bf16[384,1024]{1,0:T(8,128)(2,1)S(1)} %add.7), channel_id=1, source_target_pairs={{0,64},{64,128},{128,192},{192,0},{1,65},{65,129},{129,193},{193,1... | collective-permute-start | bytes 2359304 | tf_op jit(solution)/shard_map/ppermute | solution.py:399
  (19 other events, 377.9 us)
where the time goes:
time: 193 us; the launch traced here: 191 us
  waiting for transfers between devices  95.6 us (50%)
  Pallas kernels  46.3 us (24%)
  starting transfers between devices  40 us (21%)
  other arithmetic  4.44 us (2%)
  local copies, waits for them, and re-layouts  3.15 us (2%)
    ppermute x12, waiting for transfers between devices, move(): return lax.ppermute(a, 'y', [(i, (i + k) % ring) for i in range(ring)])  83.5 us
    ppermute x12, starting transfers between devices, move(): return lax.ppermute(a, 'y', [(i, (i + k) % ring) for i in range(ring)])  19.8 us
    all_to_all x2, starting transfers between devices, exchange(): lax.all_to_all(a, ('z', 'x'), split_axis=0, concat_axis=0, tiled=True)  19.1 us
    pallas_call x1, Pallas kernels, experts_call(): pl.pallas_call(functools.partial(experts_kernel, capacity, group, cols),...  16.2 us
    pallas_call x2, Pallas kernels, sums_call(): pl.pallas_call(functools.partial(sums_kernel, jobs), in_specs=[hbm] * 3,...  12.7 us
    all_to_all x2, waiting for transfers between devices, exchange(): lax.all_to_all(a, ('z', 'x'), split_axis=0, concat_axis=0, tiled=True)  11.8 us
    pallas_call x1, Pallas kernels, shards(): pl.pallas_call(functools.partial(before_kernel, experts, capacity), out_s...  6.16 us
    pallas_call x1, Pallas kernels, shards(): pl.pallas_call(functools.partial(after_kernel, capacity), in_specs=[vmem]...  4.65 us
  transfers between devices with their start and end apart: 23, of which 10 were waited for; matrix products, arithmetic and copies ran while one was open for 2% of the time, Pallas kernels for 10%

commit v1 on v0

--- a/solution.py
+++ b/solution.py
@@ -99,20 +99,13 @@
     for n, column in enumerate((slot0.astype(F32), slot1.astype(F32), gate0, gate1)):
         noted = jnp.where(lane == n + 1, column, noted)
     notes[...] = noted
-    values = jnp.concatenate(
-        [
-            (scaled * norm[...]).astype(BF),
-            (gate0 * d_mix).astype(BF),
-            (gate1 * d_mix).astype(BF),
-        ],
-        axis=0,
-    )
+    values = jnp.concatenate([(scaled * norm[...]).astype(BF), d_mix.astype(BF)], axis=0)
     place = iota((rows, send.shape[0]), 1)
+    weighed = jnp.where(place == slot1 + capacity, gate1, 0.0)
     spread = jnp.concatenate(
         [
             jnp.where((place == slot0) | (place == slot1), 1.0, 0.0).astype(BF),
-            jnp.where(place == slot0 + capacity, 1.0, 0.0).astype(BF),
-            jnp.where(place == slot1 + capacity, 1.0, 0.0).astype(BF),
+            jnp.where(place == slot0 + capacity, gate0, weighed).astype(BF),
         ],
         axis=0,
     )

time: 193 us -> 192 us (level)
  no operation moved by 1% of the time
where the time goes in v1:
time: 192 us; the launch traced here: 190 us
  waiting for transfers between devices  95.6 us (50%)
  Pallas kernels  45.4 us (24%)
  starting transfers between devices  40 us (21%)
  other arithmetic  4.44 us (2%)
  local copies, waits for them, and re-layouts  3.15 us (2%)
    ppermute x12, waiting for transfers between devices, move(): return lax.ppermute(a, 'y', [(i, (i + k) % ring) for i in range(ring)])  83.5 us
    ppermute x12, starting transfers between devices, move(): return lax.ppermute(a, 'y', [(i, (i + k) % ring) for i in range(ring)])  19.8 us
    all_to_all x2, starting transfers between devices, exchange(): lax.all_to_all(a, ('z', 'x'), split_axis=0, concat_axis=0, tiled=True)  19.1 us
    pallas_call x1, Pallas kernels, experts_call(): pl.pallas_call(functools.partial(experts_kernel, capacity, group, cols),...  16.2 us
    pallas_call x2, Pallas kernels, sums_call(): pl.pallas_call(functools.partial(sums_kernel, jobs), in_specs=[hbm] * 3,...  12.7 us
    all_to_all x2, waiting for transfers between devices, exchange(): lax.all_to_all(a, ('z', 'x'), split_axis=0, concat_axis=0, tiled=True)  11.8 us
    pallas_call x1, Pallas kernels, shards(): pl.pallas_call(functools.partial(before_kernel, experts, capacity), out_s...  5.29 us
    pallas_call x1, Pallas kernels, shards(): pl.pallas_call(functools.partial(after_kernel, capacity), in_specs=[vmem]...  4.66 us
  transfers between devices with their start and end apart: 23, of which 10 were waited for; matrix products, arithmetic and copies ran while one was open for 2% of the time, Pallas kernels for 10%

profile of v1, /device:TPU:26, one launch (start us, length us, event | category | flops | bytes accessed | tf_op | source)
XLA Modules:
  0.0 189.8 jit_solution(4785107676329008138)
XLA Ops:
  0.6 5.3 %before.1 = (bf16[768,2048]{1,0:T(8,128)(2,1)}, f32[96,2048]{1,0:T(8,128)}, f32[96,128]{1,0:T(8,128)}) custom-call(bf16[288,2048]{1,0:T(8,128)(2,1)} %tokens.1, bf16[288,2048]{1,0:T(8,128)(2,1)} %cotangent.1, s32[2,96]{1,0:T(2,128)} %bitcast.11, s32[2,96]{1,0:T(2,128)} %bitcast.12, f32[3,2048]{1,0:T(4,128)} %pool.3, f32[1,2048]{1,0:T(1,128)} %bitcast.7, ...), custom_call_target="tpu_custom_call" | custom-call | tf_op jit(solution)/shard_map/before/pallas_call | solution.py:417
  5.9 11.7 %all-to-all-start = ((bf16[32,24,2048]{2,1,0:T(8,128)(2,1)}), bf16[32,24,2048]{2,1,0:T(8,128)(2,1)}, u32[]{:S(2)}, u32[]{:S(2)}) async-start(bf16[32,24,2048]{2,1,0:T(8,128)(2,1)} %bitcast.9), calls=%async_computation | async-start | bytes 6291456 | tf_op jit(solution)/shard_map/all_to_all | solution.py:398
  17.6 2.4 %pack.1 = (bf16[192,2048]{1,0:T(8,128)(2,1)}, bf16[192,2048]{1,0:T(8,128)(2,1)}) custom-call(bf16[1,128,2048]{2,1,0:T(8,128)(2,1)} %w_gate.1, bf16[1,128,2048]{2,1,0:T(8,128)(2,1)} %w_up.1, bf16[1,128,2048]{2,1,0:T(8,128)(2,1)} %w_down.1), custom_call_target="tpu_custom_call" | custom-call | tf_op jit(solution)/shard_map/pack/pallas_call | solution.py:401
  20.9 2.5 %collective-permute-start = (bf16[192,2048]{1,0:T(8,128)(2,1)}, bf16[192,2048]{1,0:T(8,128)(2,1)S(1)}, u32[]{:S(2)}, u32[]{:S(2)}) collective-permute-start(bf16[192,2048]{1,0:T(8,128)(2,1)} %get-tuple-element.27), channel_id=1, source_target_pairs={{0,64},{64,128},{128,192},{192,0},{1,65},{65,129},{129,193},{193,1... | collective-permute-start | bytes 2359304 | tf_op jit(solution)/shard_map/ppermute | solution.py:392
  23.4 3.3 %collective-permute-start.1 = (bf16[192,2048]{1,0:T(8,128)(2,1)}, bf16[192,2048]{1,0:T(8,128)(2,1)S(1)}, u32[]{:S(2)}, u32[]{:S(2)}) collective-permute-start(bf16[192,2048]{1,0:T(8,128)(2,1)} %get-tuple-element.28), channel_id=1, source_target_pairs={{0,64},{64,128},{128,192},{192,0},{1,65},{65,129},{129,193},{193,1... | collective-permute-start | bytes 2359304 | tf_op jit(solution)/shard_map/ppermute | solution.py:392
  26.7 15.2 %collective-permute-done.5.refs_6_ = bf16[192,2048]{1,0:T(8,128)(2,1)S(1)} collective-permute-done((bf16[192,2048]{1,0:T(8,128)(2,1)}, bf16[192,2048]{1,0:T(8,128)(2,1)S(1)}, u32[]{:S(2)}, u32[]{:S(2)}) %collective-permute-start.5) | collective-permute-done | bytes 786464 | tf_op jit(solution)/shard_map/ppermute | solution.py:392
  41.9 3.3 %collective-permute-start.2 = (bf16[192,2048]{1,0:T(8,128)(2,1)S(1)}, bf16[192,2048]{1,0:T(8,128)(2,1)S(1)}, u32[]{:S(2)}, u32[]{:S(2)}) collective-permute-start(bf16[192,2048]{1,0:T(8,128)(2,1)S(1)} %collective-permute-done.refs_2_), channel_id=1, source_target_pairs={{0,64},{64,128},{128,192},{192,0},{1,65},{65,129},{129,193},{193,1... | collective-permute-start | bytes 2359304 | tf_op jit(solution)/shard_map/ppermute | solution.py:392
  45.2 13.1 %collective-permute-done.3.refs_7_ = bf16[192,2048]{1,0:T(8,128)(2,1)S(1)} collective-permute-done((bf16[192,2048]{1,0:T(8,128)(2,1)}, bf16[192,2048]{1,0:T(8,128)(2,1)S(1)}, u32[]{:S(2)}, u32[]{:S(2)}) %collective-permute-start.3) | collective-permute-done | bytes 786464 | tf_op jit(solution)/shard_map/ppermute | solution.py:392
  59.1 15.4 %collective-permute-done.2.refs_4_ = bf16[192,2048]{1,0:T(8,128)(2,1)S(1)} collective-permute-done((bf16[192,2048]{1,0:T(8,128)(2,1)S(1)}, bf16[192,2048]{1,0:T(8,128)(2,1)S(1)}, u32[]{:S(2)}, u32[]{:S(2)}) %collective-permute-start.2) | collective-permute-done | bytes 786464 | tf_op jit(solution)/shard_map/ppermute | solution.py:392
  74.4 4.3 %collective-permute-done.4.refs_5_ = bf16[192,2048]{1,0:T(8,128)(2,1)S(1)} collective-permute-done((bf16[192,2048]{1,0:T(8,128)(2,1)S(1)}, bf16[192,2048]{1,0:T(8,128)(2,1)S(1)}, u32[]{:S(2)}, u32[]{:S(2)}) %collective-permute-start.4) | collective-permute-done | bytes 786464 | tf_op jit(solution)/shard_map/ppermute | solution.py:392
  82.9 6.0 %all-to-all-done = bf16[32,24,2048]{2,1,0:T(8,128)(2,1)} async-done(((bf16[32,24,2048]{2,1,0:T(8,128)(2,1)}), bf16[32,24,2048]{2,1,0:T(8,128)(2,1)}, u32[]{:S(2)}, u32[]{:S(2)}) %all-to-all-start) | async-done | bytes 3145760 | tf_op jit(solution)/shard_map/all_to_all | solution.py:398
  88.9 16.2 %experts.1 = (bf16[768,2048]{1,0:T(8,128)(2,1)}, bf16[384,5632]{1,0:T(8,128)(2,1)}, bf16[3,512,384]{2,1,0:T(8,128)(2,1)}) custom-call(bf16[768,2048]{1,0:T(8,128)(2,1)} %bitcast.4.arrived, bf16[192,2048]{1,0:T(8,128)(2,1)S(1)} %get-tuple-element.48.refs_0_, bf16[192,2048]{1,0:T(8,128)(2,1)S(1)} %get-tuple-element.47.refs_1_, ...), custom_call_target="tpu_custom_call" | custom-call | flops 9663676416 | bytes 12582912 | tf_op jit(solution)/shard_map/experts/pallas_call | solution.py:212
  105.2 7.4 %all-to-all-start.1 = ((bf16[32,24,2048]{2,1,0:T(8,128)(2,1)}), bf16[32,24,2048]{2,1,0:T(8,128)(2,1)}, u32[]{:S(2)}, u32[]{:S(2)}) async-start(bf16[32,24,2048]{2,1,0:T(8,128)(2,1)} %bitcast.10), calls=%async_computation.1 | async-start | bytes 6291456 | tf_op jit(solution)/shard_map/all_to_all | solution.py:398
  112.9 6.4 %sums_far.1 = (bf16[384,1024]{1,0:T(8,128)(2,1)}, bf16[384,1024]{1,0:T(8,128)(2,1)}, bf16[384,1024]{1,0:T(8,128)(2,1)}, bf16[384,1024]{1,0:T(8,128)(2,1)}) custom-call(bf16[384,5632]{1,0:T(8,128)(2,1)} %get-tuple-element.34.packed_a, bf16[3,512,384]{2,1,0:T(8,128)(2,1)} %get-tuple-element.35.left_a, bf16[384,5632]{1,0:T(8,128)(2,1)} %collective-permute-done.14.packed_b), custom_call_target="tpu_custom_call" | custom-call | flops 2415919104 | bytes 12582912 | tf_op jit(solution)/shard_map/sums_far/pallas_call | solution.py:283
  120.0 2.5 %collective-permute-start.19 = (bf16[384,1024]{1,0:T(8,128)(2,1)}, bf16[384,1024]{1,0:T(8,128)(2,1)S(1)}, u32[]{:S(2)}, u32[]{:S(2)}) collective-permute-start(bf16[384,1024]{1,0:T(8,128)(2,1)} %get-tuple-element.43), channel_id=1, source_target_pairs={{0,64},{64,128},{128,192},{192,0},{1,65},{65,129},{129,193},{193,1... | collective-permute-start | bytes 2359304 | tf_op jit(solution)/shard_map/ppermute | solution.py:392
  122.5 3.2 %collective-permute-start.18 = (bf16[384,1024]{1,0:T(8,128)(2,1)}, bf16[384,1024]{1,0:T(8,128)(2,1)S(1)}, u32[]{:S(2)}, u32[]{:S(2)}) collective-permute-start(bf16[384,1024]{1,0:T(8,128)(2,1)} %get-tuple-element.41), channel_id=1, source_target_pairs={{0,64},{64,128},{128,192},{192,0},{1,65},{65,129},{129,193},{193,1... | collective-permute-start | bytes 2359304 | tf_op jit(solution)/shard_map/ppermute | solution.py:392
  125.8 6.3 %sums_near.1 = (bf16[384,1024]{1,0:T(8,128)(2,1)}, bf16[384,1024]{1,0:T(8,128)(2,1)}, bf16[384,1024]{1,0:T(8,128)(2,1)}, bf16[384,1024]{1,0:T(8,128)(2,1)}) custom-call(bf16[384,5632]{1,0:T(8,128)(2,1)} %get-tuple-element.34.packed_a, bf16[3,512,384]{2,1,0:T(8,128)(2,1)} %get-tuple-element.35.left_a, bf16[384,5632]{1,0:T(8,128)(2,1)} %collective-permute-done.14.packed_b), custom_call_target="tpu_custom_call" | custom-call | flops 2415919104 | bytes 12582912 | tf_op jit(solution)/shard_map/sums_near/pallas_call | solution.py:283
  132.1 9.0 %collective-permute-done.15 = bf16[384,1024]{1,0:T(8,128)(2,1)S(1)} collective-permute-done((bf16[384,1024]{1,0:T(8,128)(2,1)}, bf16[384,1024]{1,0:T(8,128)(2,1)S(1)}, u32[]{:S(2)}, u32[]{:S(2)}) %collective-permute-start.15) | collective-permute-done | bytes 786464 | tf_op jit(solution)/shard_map/ppermute | solution.py:392
  144.2 3.3 %collective-permute-start.20 = (bf16[384,1024]{1,0:T(8,128)(2,1)S(1)}, bf16[384,1024]{1,0:T(8,128)(2,1)}, u32[]{:S(2)}, u32[]{:S(2)}) collective-permute-start(bf16[384,1024]{1,0:T(8,128)(2,1)S(1)} %add.7), channel_id=1, source_target_pairs={{0,64},{64,128},{128,192},{192,0},{1,65},{65,129},{129,193},{193,1... | collective-permute-start | bytes 2359304 | tf_op jit(solution)/shard_map/ppermute | solution.py:392
  147.5 10.5 %collective-permute-done.17.q1b = bf16[384,1024]{1,0:T(8,128)(2,1)S(1)} collective-permute-done((bf16[384,1024]{1,0:T(8,128)(2,1)}, bf16[384,1024]{1,0:T(8,128)(2,1)S(1)}, u32[]{:S(2)}, u32[]{:S(2)}) %collective-permute-start.17) | collective-permute-done | bytes 786464 | tf_op jit(solution)/shard_map/ppermute | solution.py:392
  158.0 16.0 %collective-permute-done.16.q1a = bf16[384,1024]{1,0:T(8,128)(2,1)S(1)} collective-permute-done((bf16[384,1024]{1,0:T(8,128)(2,1)S(1)}, bf16[384,1024]{1,0:T(8,128)(2,1)S(1)}, u32[]{:S(2)}, u32[]{:S(2)}) %collective-permute-start.16) | collective-permute-done | bytes 786464 | tf_op jit(solution)/shard_map/ppermute | solution.py:392
  174.9 4.2 %grads.1 = (f32[1,128,2048]{2,1,0:T(8,128)}, f32[1,128,2048]{2,1,0:T(8,128)}, f32[1,128,2048]{2,1,0:T(8,128)}) custom-call(bf16[384,1024]{1,0:T(8,128)(2,1)} %get-tuple-element.36.q0a, bf16[384,1024]{1,0:T(8,128)(2,1)} %get-tuple-element.37.q0b, bf16[384,1024]{1,0:T(8,128)(2,1)} %copy-done.7, bf16[384,1024]{1,0:T(8,128)(2,1)} %copy-done.5, ...), custom_call_target="tpu_custom_call" | custom-call | tf_op jit(solution)/shard_map/grads/pallas_call | solution.py:440
  179.1 5.8 %all-to-all-done.1 = bf16[32,24,2048]{2,1,0:T(8,128)(2,1)} async-done(((bf16[32,24,2048]{2,1,0:T(8,128)(2,1)}), bf16[32,24,2048]{2,1,0:T(8,128)(2,1)}, u32[]{:S(2)}, u32[]{:S(2)}) %all-to-all-start.1) | async-done | bytes 3145760 | tf_op jit(solution)/shard_map/all_to_all | solution.py:398
  184.9 4.7 %after.1 = (bf16[288,2048]{1,0:T(8,128)(2,1)}, bf16[288,2048]{1,0:T(8,128)(2,1)}) custom-call(bf16[768,2048]{1,0:T(8,128)(2,1)} %bitcast.6.table, f32[96,2048]{1,0:T(8,128)S(1)} %copy-done, f32[96,128]{1,0:T(8,128)S(1)} %copy-done.3, f32[3,2048]{1,0:T(4,128)S(1)} %copy-done.1, f32[1,2048]{1,0:T(1,128)S(1)} %bitcast.8, f32[3,2048]{1,0:T(4,128)S(1)} %copy-done.2), custom_call_target="tpu_custom_call" | custom-call | tf_op jit(solution)/shard_map/after/pallas_call | solution.py:456
  (72 shorter events, 10.8 us)
Async XLA Ops:
  5.9 83.0 %all-to-all-start = ((bf16[32,24,2048]{2,1,0:T(8,128)(2,1)}), bf16[32,24,2048]{2,1,0:T(8,128)(2,1)}, u32[]{:S(2)}, u32[]{:S(2)}) async-start(bf16[32,24,2048]{2,1,0:T(8,128)(2,1)} %bitcast.9), calls=%async_computation | async-start | bytes 6291456 | tf_op jit(solution)/shard_map/all_to_all | solution.py:398
  20.0 3.4 %collective-permute-start.6 = (bf16[192,2048]{1,0:T(8,128)(2,1)}, bf16[192,2048]{1,0:T(8,128)(2,1)S(1)}, u32[]{:S(2)}, u32[]{:S(2)}) collective-permute-start(bf16[192,2048]{1,0:T(8,128)(2,1)} %get-tuple-element.27), channel_id=1, source_target_pairs={{0,32},{32,0},{1,33},{33,1},{2,34},{34,2},{3,35},{35,3},{4,36},{36... | collective-permute-start | bytes 2359304 | tf_op jit(solution)/shard_map/ppermute | solution.py:395
  20.1 21.8 %collective-permute-start.5 = (bf16[192,2048]{1,0:T(8,128)(2,1)}, bf16[192,2048]{1,0:T(8,128)(2,1)S(1)}, u32[]{:S(2)}, u32[]{:S(2)}) collective-permute-start(bf16[192,2048]{1,0:T(8,128)(2,1)} %get-tuple-element.27), channel_id=1, source_target_pairs={{0,192},{64,0},{128,64},{192,128},{1,193},{65,1},{129,65},{193,129... | collective-permute-start | bytes 2359304 | tf_op jit(solution)/shard_map/ppermute | solution.py:392
  20.9 21.0 %collective-permute-start = (bf16[192,2048]{1,0:T(8,128)(2,1)}, bf16[192,2048]{1,0:T(8,128)(2,1)S(1)}, u32[]{:S(2)}, u32[]{:S(2)}) collective-permute-start(bf16[192,2048]{1,0:T(8,128)(2,1)} %get-tuple-element.27), channel_id=1, source_target_pairs={{0,64},{64,128},{128,192},{192,0},{1,65},{65,129},{129,193},{193,1... | collective-permute-start | bytes 2359304 | tf_op jit(solution)/shard_map/ppermute | solution.py:392
  23.4 34.9 %collective-permute-start.3 = (bf16[192,2048]{1,0:T(8,128)(2,1)}, bf16[192,2048]{1,0:T(8,128)(2,1)S(1)}, u32[]{:S(2)}, u32[]{:S(2)}) collective-permute-start(bf16[192,2048]{1,0:T(8,128)(2,1)} %get-tuple-element.28), channel_id=1, source_target_pairs={{0,192},{64,0},{128,64},{192,128},{1,193},{65,1},{129,65},{193,129... | collective-permute-start | bytes 2359304 | tf_op jit(solution)/shard_map/ppermute | solution.py:392
  23.4 34.9 %collective-permute-start.7 = (bf16[192,2048]{1,0:T(8,128)(2,1)}, bf16[192,2048]{1,0:T(8,128)(2,1)S(1)}, u32[]{:S(2)}, u32[]{:S(2)}) collective-permute-start(bf16[192,2048]{1,0:T(8,128)(2,1)} %get-tuple-element.28), channel_id=1, source_target_pairs={{0,32},{32,0},{1,33},{33,1},{2,34},{34,2},{3,35},{35,3},{4,36},{36... | collective-permute-start | bytes 2359304 | tf_op jit(solution)/shard_map/ppermute | solution.py:395
  23.4 65.5 %copy-start.8 = (bf16[192,2048]{1,0:T(8,128)(2,1)}, bf16[192,2048]{1,0:T(8,128)(2,1)S(1)}, u32[]{:S(2)}) copy-start(bf16[192,2048]{1,0:T(8,128)(2,1)S(1)} %collective-permute-done.6.refs_8_) | copy-start | bytes 2359300
  23.4 35.1 %collective-permute-start.1 = (bf16[192,2048]{1,0:T(8,128)(2,1)}, bf16[192,2048]{1,0:T(8,128)(2,1)S(1)}, u32[]{:S(2)}, u32[]{:S(2)}) collective-permute-start(bf16[192,2048]{1,0:T(8,128)(2,1)} %get-tuple-element.28), channel_id=1, source_target_pairs={{0,64},{64,128},{128,192},{192,0},{1,65},{65,129},{129,193},{193,1... | collective-permute-start | bytes 2359304 | tf_op jit(solution)/shard_map/ppermute | solution.py:392
  41.9 17.0 %collective-permute-start.12 = (bf16[192,2048]{1,0:T(8,128)(2,1)S(1)}, bf16[192,2048]{1,0:T(8,128)(2,1)S(1)}, u32[]{:S(2)}, u32[]{:S(2)}) collective-permute-start(bf16[192,2048]{1,0:T(8,128)(2,1)S(1)} %collective-permute-done.5.refs_6_), channel_id=1, source_target_pairs={{0,32},{32,0},{1,33},{33,1},{2,34},{34,2},{3,35},{35,3},{4,36},{36... | collective-permute-start | bytes 2359304 | tf_op jit(solution)/shard_map/ppermute | solution.py:395
  41.9 32.5 %collective-permute-start.2 = (bf16[192,2048]{1,0:T(8,128)(2,1)S(1)}, bf16[192,2048]{1,0:T(8,128)(2,1)S(1)}, u32[]{:S(2)}, u32[]{:S(2)}) collective-permute-start(bf16[192,2048]{1,0:T(8,128)(2,1)S(1)} %collective-permute-done.refs_2_), channel_id=1, source_target_pairs={{0,64},{64,128},{128,192},{192,0},{1,65},{65,129},{129,193},{193,1... | collective-permute-start | bytes 2359304 | tf_op jit(solution)/shard_map/ppermute | solution.py:392
  58.3 20.4 %collective-permute-start.4 = (bf16[192,2048]{1,0:T(8,128)(2,1)S(1)}, bf16[192,2048]{1,0:T(8,128)(2,1)S(1)}, u32[]{:S(2)}, u32[]{:S(2)}) collective-permute-start(bf16[192,2048]{1,0:T(8,128)(2,1)S(1)} %collective-permute-done.3.refs_7_), channel_id=1, source_target_pairs={{0,192},{64,0},{128,64},{192,128},{1,193},{65,1},{129,65},{193,129... | collective-permute-start | bytes 2359304 | tf_op jit(solution)/shard_map/ppermute | solution.py:392
  58.3 22.2 %collective-permute-start.8 = (bf16[192,2048]{1,0:T(8,128)(2,1)S(1)}, bf16[192,2048]{1,0:T(8,128)(2,1)S(1)}, u32[]{:S(2)}, u32[]{:S(2)}) collective-permute-start(bf16[192,2048]{1,0:T(8,128)(2,1)S(1)} %collective-permute-done.refs_2_), channel_id=1, source_target_pairs={{0,32},{32,0},{1,33},{33,1},{2,34},{34,2},{3,35},{35,3},{4,36},{36... | collective-permute-start | bytes 2359304 | tf_op jit(solution)/shard_map/ppermute | solution.py:395
  58.5 22.1 %collective-permute-start.13 = (bf16[192,2048]{1,0:T(8,128)(2,1)S(1)}, bf16[192,2048]{1,0:T(8,128)(2,1)S(1)}, u32[]{:S(2)}, u32[]{:S(2)}) collective-permute-start(bf16[192,2048]{1,0:T(8,128)(2,1)S(1)} %collective-permute-done.3.refs_7_), channel_id=1, source_target_pairs={{0,32},{32,0},{1,33},{33,1},{2,34},{34,2},{3,35},{35,3},{4,36},{36... | collective-permute-start | bytes 2359304 | tf_op jit(solution)/shard_map/ppermute | solution.py:395
  59.0 21.7 %collective-permute-start.9 = (bf16[192,2048]{1,0:T(8,128)(2,1)S(1)}, bf16[192,2048]{1,0:T(8,128)(2,1)S(1)}, u32[]{:S(2)}, u32[]{:S(2)}) collective-permute-start(bf16[192,2048]{1,0:T(8,128)(2,1)S(1)} %collective-permute-done.1.refs_3_), channel_id=1, source_target_pairs={{0,32},{32,0},{1,33},{33,1},{2,34},{34,2},{3,35},{35,3},{4,36},{36... | collective-permute-start | bytes 2359304 | tf_op jit(solution)/shard_map/ppermute | solution.py:395
  74.4 6.2 %collective-permute-start.10 = (bf16[192,2048]{1,0:T(8,128)(2,1)S(1)}, bf16[192,2048]{1,0:T(8,128)(2,1)S(1)}, u32[]{:S(2)}, u32[]{:S(2)}) collective-permute-start(bf16[192,2048]{1,0:T(8,128)(2,1)S(1)} %collective-permute-done.2.refs_4_), channel_id=1, source_target_pairs={{0,32},{32,0},{1,33},{33,1},{2,34},{34,2},{3,35},{35,3},{4,36},{36... | collective-permute-start | bytes 2359304 | tf_op jit(solution)/shard_map/ppermute | solution.py:395
  78.7 4.1 %collective-permute-start.11 = (bf16[192,2048]{1,0:T(8,128)(2,1)S(1)}, bf16[192,2048]{1,0:T(8,128)(2,1)}, u32[]{:S(2)}, u32[]{:S(2)}) collective-permute-start(bf16[192,2048]{1,0:T(8,128)(2,1)S(1)} %collective-permute-done.4.refs_5_), channel_id=1, source_target_pairs={{0,32},{32,0},{1,33},{33,1},{2,34},{34,2},{3,35},{35,3},{4,36},{36... | collective-permute-start | bytes 2359304 | tf_op jit(solution)/shard_map/ppermute | solution.py:395
  105.1 7.8 %collective-permute-start.14 = (bf16[384,5632]{1,0:T(8,128)(2,1)}, bf16[384,5632]{1,0:T(8,128)(2,1)}, u32[]{:S(2)}, u32[]{:S(2)}) collective-permute-start(bf16[384,5632]{1,0:T(8,128)(2,1)} %get-tuple-element.34.packed_a), channel_id=1, source_target_pairs={{0,32},{32,0},{1,33},{33,1},{2,34},{34,2},{3,35},{35,3},{4,36},{36... | collective-permute-start | bytes 12976136 | tf_op jit(solution)/shard_map/ppermute | solution.py:395
  105.2 79.7 %all-to-all-start.1 = ((bf16[32,24,2048]{2,1,0:T(8,128)(2,1)}), bf16[32,24,2048]{2,1,0:T(8,128)(2,1)}, u32[]{:S(2)}, u32[]{:S(2)}) async-start(bf16[32,24,2048]{2,1,0:T(8,128)(2,1)} %bitcast.10), calls=%async_computation.1 | async-start | bytes 6291456 | tf_op jit(solution)/shard_map/all_to_all | solution.py:398
  119.2 21.9 %collective-permute-start.15 = (bf16[384,1024]{1,0:T(8,128)(2,1)}, bf16[384,1024]{1,0:T(8,128)(2,1)S(1)}, u32[]{:S(2)}, u32[]{:S(2)}) collective-permute-start(bf16[384,1024]{1,0:T(8,128)(2,1)} %get-tuple-element.39), channel_id=1, source_target_pairs={{0,192},{64,0},{128,64},{192,128},{1,193},{65,1},{129,65},{193,129... | collective-permute-start | bytes 2359304 | tf_op jit(solution)/shard_map/ppermute | solution.py:392
  120.0 22.6 %collective-permute-start.19 = (bf16[384,1024]{1,0:T(8,128)(2,1)}, bf16[384,1024]{1,0:T(8,128)(2,1)S(1)}, u32[]{:S(2)}, u32[]{:S(2)}) collective-permute-start(bf16[384,1024]{1,0:T(8,128)(2,1)} %get-tuple-element.43), channel_id=1, source_target_pairs={{0,64},{64,128},{128,192},{192,0},{1,65},{65,129},{129,193},{193,1... | collective-permute-start | bytes 2359304 | tf_op jit(solution)/shard_map/ppermute | solution.py:392
  122.5 35.4 %collective-permute-start.17 = (bf16[384,1024]{1,0:T(8,128)(2,1)}, bf16[384,1024]{1,0:T(8,128)(2,1)S(1)}, u32[]{:S(2)}, u32[]{:S(2)}) collective-permute-start(bf16[384,1024]{1,0:T(8,128)(2,1)} %get-tuple-element.40), channel_id=1, source_target_pairs={{0,192},{64,0},{128,64},{192,128},{1,193},{65,1},{129,65},{193,129... | collective-permute-start | bytes 2359304 | tf_op jit(solution)/shard_map/ppermute | solution.py:392
  122.5 35.4 %collective-permute-start.18 = (bf16[384,1024]{1,0:T(8,128)(2,1)}, bf16[384,1024]{1,0:T(8,128)(2,1)S(1)}, u32[]{:S(2)}, u32[]{:S(2)}) collective-permute-start(bf16[384,1024]{1,0:T(8,128)(2,1)} %get-tuple-element.41), channel_id=1, source_target_pairs={{0,64},{64,128},{128,192},{192,0},{1,65},{65,129},{129,193},{193,1... | collective-permute-start | bytes 2359304 | tf_op jit(solution)/shard_map/ppermute | solution.py:392
  142.6 31.5 %collective-permute-start.16 = (bf16[384,1024]{1,0:T(8,128)(2,1)S(1)}, bf16[384,1024]{1,0:T(8,128)(2,1)S(1)}, u32[]{:S(2)}, u32[]{:S(2)}) collective-permute-start(bf16[384,1024]{1,0:T(8,128)(2,1)S(1)} %add.6), channel_id=1, source_target_pairs={{0,192},{64,0},{128,64},{192,128},{1,193},{65,1},{129,65},{193,129... | collective-permute-start | bytes 2359304 | tf_op jit(solution)/shard_map/ppermute | solution.py:392
  144.2 29.8 %collective-permute-start.20 = (bf16[384,1024]{1,0:T(8,128)(2,1)S(1)}, bf16[384,1024]{1,0:T(8,128)(2,1)}, u32[]{:S(2)}, u32[]{:S(2)}) collective-permute-start(bf16[384,1024]{1,0:T(8,128)(2,1)S(1)} %add.7), channel_id=1, source_target_pairs={{0,64},{64,128},{128,192},{192,0},{1,65},{65,129},{129,193},{193,1... | collective-permute-start | bytes 2359304 | tf_op jit(solution)/shard_map/ppermute | solution.py:392
  (19 other events, 377.9 us)

commit v2 on v1

--- a/solution.py
+++ b/solution.py
@@ -10,6 +10,7 @@
 BF = jnp.bfloat16
 F32 = jnp.float32
 MIB = 1024 * 1024
+BLOCKS = 4
 EDGE_LIMIT = 60 * MIB
 AFTER_LIMIT = 52 * MIB
 EXPERTS_LIMIT = 51 * MIB
@@ -71,7 +72,7 @@
         copy.wait()
 
 
-def before_kernel(experts, capacity, tokens, cotangent, ids, votes, pool, norm, gain, send, scaled_out, notes):
+def before_kernel(experts, capacity, tokens, cotangent, ids, votes, pool, norm, gain, send, scaled_out, notes, kept, out, sem):
     rows = ids.shape[1]
     factor = tokens.shape[0] // rows
     slot0, slot1, gate0, gate1 = slots_and_gates(ids, votes, experts, capacity)
@@ -93,14 +94,16 @@
     d_mix = jnp.concatenate(mixes, axis=0)
     inv = lax.rsqrt(jnp.mean(short * short, axis=1, keepdims=True) + 1e-06)
     scaled = short * inv
-    scaled_out[...] = scaled
+    kept[...] = scaled
+    copies = [pltpu.make_async_copy(kept, scaled_out, sem.at[0])]
+    copies[0].start()
     lane = iota(notes.shape, 1)
     noted = inv
     for n, column in enumerate((slot0.astype(F32), slot1.astype(F32), gate0, gate1)):
         noted = jnp.where(lane == n + 1, column, noted)
     notes[...] = noted
     values = jnp.concatenate([(scaled * norm[...]).astype(BF), d_mix.astype(BF)], axis=0)
-    place = iota((rows, send.shape[0]), 1)
+    place = iota((rows, out.shape[0]), 1)
     weighed = jnp.where(place == slot1 + capacity, gate1, 0.0)
     spread = jnp.concatenate(
         [
@@ -109,7 +112,16 @@
         ],
         axis=0,
     )
-    send[...] = tn(spread, values).astype(BF)
+    blocks = sem.shape[0] - 1
+    cols = out.shape[1] // blocks
+    for n in range(blocks):
+        at = slice(n * cols, (n + 1) * cols)
+        out[:, at] = tn(spread, values[:, at]).astype(BF)
+        copy = pltpu.make_async_copy(out.at[:, pl.ds(n * cols, cols)], send.at[:, pl.ds(n * cols, cols)], sem.at[1 + n])
+        copy.start()
+        copies.append(copy)
+    for copy in copies:
+        copy.wait()
 
 
 def split_matrix(rows, capacity):
@@ -416,11 +428,14 @@
 
     send, scaled, notes = pl.pallas_call(
         functools.partial(before_kernel, experts, capacity),
+        in_specs=[vmem] * 7,
+        out_specs=[hbm, hbm, vmem],
         out_shape=(
             jax.ShapeDtypeStruct((slots, width), BF),
             jax.ShapeDtypeStruct((rows, width), F32),
             jax.ShapeDtypeStruct((rows, 128), F32),
         ),
+        scratch_shapes=[pltpu.VMEM((rows, width), F32), pltpu.VMEM((slots, width), BF), pltpu.SemaphoreType.DMA((BLOCKS + 1,))],
         compiler_params=params,
         name="before",
     )(tokens, cotangent, ids, counts, pool_weight, norm, up_gain)

time: 192 us -> 192 us (level)
  no operation moved by 1% of the time
where the time goes in v2:
time: 192 us; the launch traced here: 190 us
  waiting for transfers between devices  95.6 us (50%)
  Pallas kernels  45.7 us (24%)
  starting transfers between devices  40 us (21%)
  other arithmetic  4.44 us (2%)
  local copies, waits for them, and re-layouts  3.15 us (2%)
    ppermute x12, waiting for transfers between devices, move(): return lax.ppermute(a, 'y', [(i, (i + k) % ring) for i in range(ring)])  83.5 us
    ppermute x12, starting transfers between devices, move(): return lax.ppermute(a, 'y', [(i, (i + k) % ring) for i in range(ring)])  19.8 us
    all_to_all x2, starting transfers between devices, exchange(): lax.all_to_all(a, ('z', 'x'), split_axis=0, concat_axis=0, tiled=True)  19.1 us
    pallas_call x1, Pallas kernels, experts_call(): pl.pallas_call(functools.partial(experts_kernel, capacity, group, cols),...  16.2 us
    pallas_call x2, Pallas kernels, sums_call(): pl.pallas_call(functools.partial(sums_kernel, jobs), in_specs=[hbm] * 3,...  12.7 us
    all_to_all x2, waiting for transfers between devices, exchange(): lax.all_to_all(a, ('z', 'x'), split_axis=0, concat_axis=0, tiled=True)  11.8 us
    pallas_call x1, Pallas kernels, shards(): pl.pallas_call(functools.partial(before_kernel, experts, capacity), in_sp...  5.54 us
    pallas_call x1, Pallas kernels, shards(): pl.pallas_call(functools.partial(after_kernel, capacity), in_specs=[vmem]...  4.66 us
  transfers between devices with their start and end apart: 23, of which 10 were waited for; matrix products, arithmetic and copies ran while one was open for 2% of the time, Pallas kernels for 10%

profile of v2, /device:TPU:26, one launch (start us, length us, event | category | flops | bytes accessed | tf_op | source)
XLA Modules:
  0.0 190.0 jit_solution(2960454186902852913)
XLA Ops:
  0.6 5.5 %before.1 = (bf16[768,2048]{1,0:T(8,128)(2,1)}, f32[96,2048]{1,0:T(8,128)}, f32[96,128]{1,0:T(8,128)}) custom-call(bf16[288,2048]{1,0:T(8,128)(2,1)} %tokens.1, bf16[288,2048]{1,0:T(8,128)(2,1)} %cotangent.1, s32[2,96]{1,0:T(2,128)} %bitcast.11, s32[2,96]{1,0:T(2,128)} %bitcast.12, f32[3,2048]{1,0:T(4,128)} %pool.3, f32[1,2048]{1,0:T(1,128)} %bitcast.7, ...), custom_call_target="tpu_custom_call" | custom-call | tf_op jit(solution)/shard_map/before/pallas_call | solution.py:429
  6.2 11.7 %all-to-all-start = ((bf16[32,24,2048]{2,1,0:T(8,128)(2,1)}), bf16[32,24,2048]{2,1,0:T(8,128)(2,1)}, u32[]{:S(2)}, u32[]{:S(2)}) async-start(bf16[32,24,2048]{2,1,0:T(8,128)(2,1)} %bitcast.9), calls=%async_computation | async-start | bytes 6291456 | tf_op jit(solution)/shard_map/all_to_all | solution.py:410
  17.9 2.4 %pack.1 = (bf16[192,2048]{1,0:T(8,128)(2,1)}, bf16[192,2048]{1,0:T(8,128)(2,1)}) custom-call(bf16[1,128,2048]{2,1,0:T(8,128)(2,1)} %w_gate.1, bf16[1,128,2048]{2,1,0:T(8,128)(2,1)} %w_up.1, bf16[1,128,2048]{2,1,0:T(8,128)(2,1)} %w_down.1), custom_call_target="tpu_custom_call" | custom-call | tf_op jit(solution)/shard_map/pack/pallas_call | solution.py:413
  21.2 2.5 %collective-permute-start = (bf16[192,2048]{1,0:T(8,128)(2,1)}, bf16[192,2048]{1,0:T(8,128)(2,1)S(1)}, u32[]{:S(2)}, u32[]{:S(2)}) collective-permute-start(bf16[192,2048]{1,0:T(8,128)(2,1)} %get-tuple-element.27), channel_id=1, source_target_pairs={{0,64},{64,128},{128,192},{192,0},{1,65},{65,129},{129,193},{193,1... | collective-permute-start | bytes 2359304 | tf_op jit(solution)/shard_map/ppermute | solution.py:404
  23.7 3.3 %collective-permute-start.1 = (bf16[192,2048]{1,0:T(8,128)(2,1)}, bf16[192,2048]{1,0:T(8,128)(2,1)S(1)}, u32[]{:S(2)}, u32[]{:S(2)}) collective-permute-start(bf16[192,2048]{1,0:T(8,128)(2,1)} %get-tuple-element.28), channel_id=1, source_target_pairs={{0,64},{64,128},{128,192},{192,0},{1,65},{65,129},{129,193},{193,1... | collective-permute-start | bytes 2359304 | tf_op jit(solution)/shard_map/ppermute | solution.py:404
  27.0 15.2 %collective-permute-done.5.refs_6_ = bf16[192,2048]{1,0:T(8,128)(2,1)S(1)} collective-permute-done((bf16[192,2048]{1,0:T(8,128)(2,1)}, bf16[192,2048]{1,0:T(8,128)(2,1)S(1)}, u32[]{:S(2)}, u32[]{:S(2)}) %collective-permute-start.5) | collective-permute-done | bytes 786464 | tf_op jit(solution)/shard_map/ppermute | solution.py:404
  42.2 3.3 %collective-permute-start.2 = (bf16[192,2048]{1,0:T(8,128)(2,1)S(1)}, bf16[192,2048]{1,0:T(8,128)(2,1)S(1)}, u32[]{:S(2)}, u32[]{:S(2)}) collective-permute-start(bf16[192,2048]{1,0:T(8,128)(2,1)S(1)} %collective-permute-done.refs_2_), channel_id=1, source_target_pairs={{0,64},{64,128},{128,192},{192,0},{1,65},{65,129},{129,193},{193,1... | collective-permute-start | bytes 2359304 | tf_op jit(solution)/shard_map/ppermute | solution.py:404
  45.5 13.1 %collective-permute-done.3.refs_7_ = bf16[192,2048]{1,0:T(8,128)(2,1)S(1)} collective-permute-done((bf16[192,2048]{1,0:T(8,128)(2,1)}, bf16[192,2048]{1,0:T(8,128)(2,1)S(1)}, u32[]{:S(2)}, u32[]{:S(2)}) %collective-permute-start.3) | collective-permute-done | bytes 786464 | tf_op jit(solution)/shard_map/ppermute | solution.py:404
  59.3 15.4 %collective-permute-done.2.refs_4_ = bf16[192,2048]{1,0:T(8,128)(2,1)S(1)} collective-permute-done((bf16[192,2048]{1,0:T(8,128)(2,1)S(1)}, bf16[192,2048]{1,0:T(8,128)(2,1)S(1)}, u32[]{:S(2)}, u32[]{:S(2)}) %collective-permute-start.2) | collective-permute-done | bytes 786464 | tf_op jit(solution)/shard_map/ppermute | solution.py:404
  74.7 4.3 %collective-permute-done.4.refs_5_ = bf16[192,2048]{1,0:T(8,128)(2,1)S(1)} collective-permute-done((bf16[192,2048]{1,0:T(8,128)(2,1)S(1)}, bf16[192,2048]{1,0:T(8,128)(2,1)S(1)}, u32[]{:S(2)}, u32[]{:S(2)}) %collective-permute-start.4) | collective-permute-done | bytes 786464 | tf_op jit(solution)/shard_map/ppermute | solution.py:404
  83.1 6.0 %all-to-all-done = bf16[32,24,2048]{2,1,0:T(8,128)(2,1)} async-done(((bf16[32,24,2048]{2,1,0:T(8,128)(2,1)}), bf16[32,24,2048]{2,1,0:T(8,128)(2,1)}, u32[]{:S(2)}, u32[]{:S(2)}) %all-to-all-start) | async-done | bytes 3145760 | tf_op jit(solution)/shard_map/all_to_all | solution.py:410
  89.2 16.2 %experts.1 = (bf16[768,2048]{1,0:T(8,128)(2,1)}, bf16[384,5632]{1,0:T(8,128)(2,1)}, bf16[3,512,384]{2,1,0:T(8,128)(2,1)}) custom-call(bf16[768,2048]{1,0:T(8,128)(2,1)} %bitcast.4.arrived, bf16[192,2048]{1,0:T(8,128)(2,1)S(1)} %get-tuple-element.48.refs_0_, bf16[192,2048]{1,0:T(8,128)(2,1)S(1)} %get-tuple-element.47.refs_1_, ...), custom_call_target="tpu_custom_call" | custom-call | flops 9663676416 | bytes 12582912 | tf_op jit(solution)/shard_map/experts/pallas_call | solution.py:224
  105.4 7.4 %all-to-all-start.1 = ((bf16[32,24,2048]{2,1,0:T(8,128)(2,1)}), bf16[32,24,2048]{2,1,0:T(8,128)(2,1)}, u32[]{:S(2)}, u32[]{:S(2)}) async-start(bf16[32,24,2048]{2,1,0:T(8,128)(2,1)} %bitcast.10), calls=%async_computation.1 | async-start | bytes 6291456 | tf_op jit(solution)/shard_map/all_to_all | solution.py:410
  113.1 6.4 %sums_far.1 = (bf16[384,1024]{1,0:T(8,128)(2,1)}, bf16[384,1024]{1,0:T(8,128)(2,1)}, bf16[384,1024]{1,0:T(8,128)(2,1)}, bf16[384,1024]{1,0:T(8,128)(2,1)}) custom-call(bf16[384,5632]{1,0:T(8,128)(2,1)} %get-tuple-element.34.packed_a, bf16[3,512,384]{2,1,0:T(8,128)(2,1)} %get-tuple-element.35.left_a, bf16[384,5632]{1,0:T(8,128)(2,1)} %collective-permute-done.14.packed_b), custom_call_target="tpu_custom_call" | custom-call | flops 2415919104 | bytes 12582912 | tf_op jit(solution)/shard_map/sums_far/pallas_call | solution.py:295
  120.3 2.5 %collective-permute-start.19 = (bf16[384,1024]{1,0:T(8,128)(2,1)}, bf16[384,1024]{1,0:T(8,128)(2,1)S(1)}, u32[]{:S(2)}, u32[]{:S(2)}) collective-permute-start(bf16[384,1024]{1,0:T(8,128)(2,1)} %get-tuple-element.43), channel_id=1, source_target_pairs={{0,64},{64,128},{128,192},{192,0},{1,65},{65,129},{129,193},{193,1... | collective-permute-start | bytes 2359304 | tf_op jit(solution)/shard_map/ppermute | solution.py:404
  122.8 3.2 %collective-permute-start.18 = (bf16[384,1024]{1,0:T(8,128)(2,1)}, bf16[384,1024]{1,0:T(8,128)(2,1)S(1)}, u32[]{:S(2)}, u32[]{:S(2)}) collective-permute-start(bf16[384,1024]{1,0:T(8,128)(2,1)} %get-tuple-element.41), channel_id=1, source_target_pairs={{0,64},{64,128},{128,192},{192,0},{1,65},{65,129},{129,193},{193,1... | collective-permute-start | bytes 2359304 | tf_op jit(solution)/shard_map/ppermute | solution.py:404
  126.0 6.3 %sums_near.1 = (bf16[384,1024]{1,0:T(8,128)(2,1)}, bf16[384,1024]{1,0:T(8,128)(2,1)}, bf16[384,1024]{1,0:T(8,128)(2,1)}, bf16[384,1024]{1,0:T(8,128)(2,1)}) custom-call(bf16[384,5632]{1,0:T(8,128)(2,1)} %get-tuple-element.34.packed_a, bf16[3,512,384]{2,1,0:T(8,128)(2,1)} %get-tuple-element.35.left_a, bf16[384,5632]{1,0:T(8,128)(2,1)} %collective-permute-done.14.packed_b), custom_call_target="tpu_custom_call" | custom-call | flops 2415919104 | bytes 12582912 | tf_op jit(solution)/shard_map/sums_near/pallas_call | solution.py:295
  132.4 9.0 %collective-permute-done.15 = bf16[384,1024]{1,0:T(8,128)(2,1)S(1)} collective-permute-done((bf16[384,1024]{1,0:T(8,128)(2,1)}, bf16[384,1024]{1,0:T(8,128)(2,1)S(1)}, u32[]{:S(2)}, u32[]{:S(2)}) %collective-permute-start.15) | collective-permute-done | bytes 786464 | tf_op jit(solution)/shard_map/ppermute | solution.py:404
  144.5 3.3 %collective-permute-start.20 = (bf16[384,1024]{1,0:T(8,128)(2,1)S(1)}, bf16[384,1024]{1,0:T(8,128)(2,1)}, u32[]{:S(2)}, u32[]{:S(2)}) collective-permute-start(bf16[384,1024]{1,0:T(8,128)(2,1)S(1)} %add.7), channel_id=1, source_target_pairs={{0,64},{64,128},{128,192},{192,0},{1,65},{65,129},{129,193},{193,1... | collective-permute-start | bytes 2359304 | tf_op jit(solution)/shard_map/ppermute | solution.py:404
  147.7 10.5 %collective-permute-done.17.q1b = bf16[384,1024]{1,0:T(8,128)(2,1)S(1)} collective-permute-done((bf16[384,1024]{1,0:T(8,128)(2,1)}, bf16[384,1024]{1,0:T(8,128)(2,1)S(1)}, u32[]{:S(2)}, u32[]{:S(2)}) %collective-permute-start.17) | collective-permute-done | bytes 786464 | tf_op jit(solution)/shard_map/ppermute | solution.py:404
  158.2 16.0 %collective-permute-done.16.q1a = bf16[384,1024]{1,0:T(8,128)(2,1)S(1)} collective-permute-done((bf16[384,1024]{1,0:T(8,128)(2,1)S(1)}, bf16[384,1024]{1,0:T(8,128)(2,1)S(1)}, u32[]{:S(2)}, u32[]{:S(2)}) %collective-permute-start.16) | collective-permute-done | bytes 786464 | tf_op jit(solution)/shard_map/ppermute | solution.py:404
  175.1 4.2 %grads.1 = (f32[1,128,2048]{2,1,0:T(8,128)}, f32[1,128,2048]{2,1,0:T(8,128)}, f32[1,128,2048]{2,1,0:T(8,128)}) custom-call(bf16[384,1024]{1,0:T(8,128)(2,1)} %get-tuple-element.36.q0a, bf16[384,1024]{1,0:T(8,128)(2,1)} %get-tuple-element.37.q0b, bf16[384,1024]{1,0:T(8,128)(2,1)} %copy-done.7, bf16[384,1024]{1,0:T(8,128)(2,1)} %copy-done.5, ...), custom_call_target="tpu_custom_call" | custom-call | tf_op jit(solution)/shard_map/grads/pallas_call | solution.py:455
  179.4 5.8 %all-to-all-done.1 = bf16[32,24,2048]{2,1,0:T(8,128)(2,1)} async-done(((bf16[32,24,2048]{2,1,0:T(8,128)(2,1)}), bf16[32,24,2048]{2,1,0:T(8,128)(2,1)}, u32[]{:S(2)}, u32[]{:S(2)}) %all-to-all-start.1) | async-done | bytes 3145760 | tf_op jit(solution)/shard_map/all_to_all | solution.py:410
  185.2 4.7 %after.1 = (bf16[288,2048]{1,0:T(8,128)(2,1)}, bf16[288,2048]{1,0:T(8,128)(2,1)}) custom-call(bf16[768,2048]{1,0:T(8,128)(2,1)} %bitcast.6.table, f32[96,2048]{1,0:T(8,128)S(1)} %copy-done, f32[96,128]{1,0:T(8,128)S(1)} %copy-done.3, f32[3,2048]{1,0:T(4,128)S(1)} %copy-done.1, f32[1,2048]{1,0:T(1,128)S(1)} %bitcast.8, f32[3,2048]{1,0:T(4,128)S(1)} %copy-done.2), custom_call_target="tpu_custom_call" | custom-call | tf_op jit(solution)/shard_map/after/pallas_call | solution.py:471
  (72 shorter events, 10.8 us)
Async XLA Ops:
  6.2 83.0 %all-to-all-start = ((bf16[32,24,2048]{2,1,0:T(8,128)(2,1)}), bf16[32,24,2048]{2,1,0:T(8,128)(2,1)}, u32[]{:S(2)}, u32[]{:S(2)}) async-start(bf16[32,24,2048]{2,1,0:T(8,128)(2,1)} %bitcast.9), calls=%async_computation | async-start | bytes 6291456 | tf_op jit(solution)/shard_map/all_to_all | solution.py:410
  20.3 3.4 %collective-permute-start.6 = (bf16[192,2048]{1,0:T(8,128)(2,1)}, bf16[192,2048]{1,0:T(8,128)(2,1)S(1)}, u32[]{:S(2)}, u32[]{:S(2)}) collective-permute-start(bf16[192,2048]{1,0:T(8,128)(2,1)} %get-tuple-element.27), channel_id=1, source_target_pairs={{0,32},{32,0},{1,33},{33,1},{2,34},{34,2},{3,35},{35,3},{4,36},{36... | collective-permute-start | bytes 2359304 | tf_op jit(solution)/shard_map/ppermute | solution.py:407
  20.4 21.8 %collective-permute-start.5 = (bf16[192,2048]{1,0:T(8,128)(2,1)}, bf16[192,2048]{1,0:T(8,128)(2,1)S(1)}, u32[]{:S(2)}, u32[]{:S(2)}) collective-permute-start(bf16[192,2048]{1,0:T(8,128)(2,1)} %get-tuple-element.27), channel_id=1, source_target_pairs={{0,192},{64,0},{128,64},{192,128},{1,193},{65,1},{129,65},{193,129... | collective-permute-start | bytes 2359304 | tf_op jit(solution)/shard_map/ppermute | solution.py:404
  21.2 21.0 %collective-permute-start = (bf16[192,2048]{1,0:T(8,128)(2,1)}, bf16[192,2048]{1,0:T(8,128)(2,1)S(1)}, u32[]{:S(2)}, u32[]{:S(2)}) collective-permute-start(bf16[192,2048]{1,0:T(8,128)(2,1)} %get-tuple-element.27), channel_id=1, source_target_pairs={{0,64},{64,128},{128,192},{192,0},{1,65},{65,129},{129,193},{193,1... | collective-permute-start | bytes 2359304 | tf_op jit(solution)/shard_map/ppermute | solution.py:404
  23.7 34.9 %collective-permute-start.3 = (bf16[192,2048]{1,0:T(8,128)(2,1)}, bf16[192,2048]{1,0:T(8,128)(2,1)S(1)}, u32[]{:S(2)}, u32[]{:S(2)}) collective-permute-start(bf16[192,2048]{1,0:T(8,128)(2,1)} %get-tuple-element.28), channel_id=1, source_target_pairs={{0,192},{64,0},{128,64},{192,128},{1,193},{65,1},{129,65},{193,129... | collective-permute-start | bytes 2359304 | tf_op jit(solution)/shard_map/ppermute | solution.py:404
  23.7 34.9 %collective-permute-start.7 = (bf16[192,2048]{1,0:T(8,128)(2,1)}, bf16[192,2048]{1,0:T(8,128)(2,1)S(1)}, u32[]{:S(2)}, u32[]{:S(2)}) collective-permute-start(bf16[192,2048]{1,0:T(8,128)(2,1)} %get-tuple-element.28), channel_id=1, source_target_pairs={{0,32},{32,0},{1,33},{33,1},{2,34},{34,2},{3,35},{35,3},{4,36},{36... | collective-permute-start | bytes 2359304 | tf_op jit(solution)/shard_map/ppermute | solution.py:407
  23.7 65.5 %copy-start.8 = (bf16[192,2048]{1,0:T(8,128)(2,1)}, bf16[192,2048]{1,0:T(8,128)(2,1)S(1)}, u32[]{:S(2)}) copy-start(bf16[192,2048]{1,0:T(8,128)(2,1)S(1)} %collective-permute-done.6.refs_8_) | copy-start | bytes 2359300
  23.7 35.1 %collective-permute-start.1 = (bf16[192,2048]{1,0:T(8,128)(2,1)}, bf16[192,2048]{1,0:T(8,128)(2,1)S(1)}, u32[]{:S(2)}, u32[]{:S(2)}) collective-permute-start(bf16[192,2048]{1,0:T(8,128)(2,1)} %get-tuple-element.28), channel_id=1, source_target_pairs={{0,64},{64,128},{128,192},{192,0},{1,65},{65,129},{129,193},{193,1... | collective-permute-start | bytes 2359304 | tf_op jit(solution)/shard_map/ppermute | solution.py:404
  42.2 17.0 %collective-permute-start.12 = (bf16[192,2048]{1,0:T(8,128)(2,1)S(1)}, bf16[192,2048]{1,0:T(8,128)(2,1)S(1)}, u32[]{:S(2)}, u32[]{:S(2)}) collective-permute-start(bf16[192,2048]{1,0:T(8,128)(2,1)S(1)} %collective-permute-done.5.refs_6_), channel_id=1, source_target_pairs={{0,32},{32,0},{1,33},{33,1},{2,34},{34,2},{3,35},{35,3},{4,36},{36... | collective-permute-start | bytes 2359304 | tf_op jit(solution)/shard_map/ppermute | solution.py:407
  42.2 32.5 %collective-permute-start.2 = (bf16[192,2048]{1,0:T(8,128)(2,1)S(1)}, bf16[192,2048]{1,0:T(8,128)(2,1)S(1)}, u32[]{:S(2)}, u32[]{:S(2)}) collective-permute-start(bf16[192,2048]{1,0:T(8,128)(2,1)S(1)} %collective-permute-done.refs_2_), channel_id=1, source_target_pairs={{0,64},{64,128},{128,192},{192,0},{1,65},{65,129},{129,193},{193,1... | collective-permute-start | bytes 2359304 | tf_op jit(solution)/shard_map/ppermute | solution.py:404
  58.6 20.4 %collective-permute-start.4 = (bf16[192,2048]{1,0:T(8,128)(2,1)S(1)}, bf16[192,2048]{1,0:T(8,128)(2,1)S(1)}, u32[]{:S(2)}, u32[]{:S(2)}) collective-permute-start(bf16[192,2048]{1,0:T(8,128)(2,1)S(1)} %collective-permute-done.3.refs_7_), channel_id=1, source_target_pairs={{0,192},{64,0},{128,64},{192,128},{1,193},{65,1},{129,65},{193,129... | collective-permute-start | bytes 2359304 | tf_op jit(solution)/shard_map/ppermute | solution.py:404
  58.6 22.2 %collective-permute-start.8 = (bf16[192,2048]{1,0:T(8,128)(2,1)S(1)}, bf16[192,2048]{1,0:T(8,128)(2,1)S(1)}, u32[]{:S(2)}, u32[]{:S(2)}) collective-permute-start(bf16[192,2048]{1,0:T(8,128)(2,1)S(1)} %collective-permute-done.refs_2_), channel_id=1, source_target_pairs={{0,32},{32,0},{1,33},{33,1},{2,34},{34,2},{3,35},{35,3},{4,36},{36... | collective-permute-start | bytes 2359304 | tf_op jit(solution)/shard_map/ppermute | solution.py:407
  58.7 22.1 %collective-permute-start.13 = (bf16[192,2048]{1,0:T(8,128)(2,1)S(1)}, bf16[192,2048]{1,0:T(8,128)(2,1)S(1)}, u32[]{:S(2)}, u32[]{:S(2)}) collective-permute-start(bf16[192,2048]{1,0:T(8,128)(2,1)S(1)} %collective-permute-done.3.refs_7_), channel_id=1, source_target_pairs={{0,32},{32,0},{1,33},{33,1},{2,34},{34,2},{3,35},{35,3},{4,36},{36... | collective-permute-start | bytes 2359304 | tf_op jit(solution)/shard_map/ppermute | solution.py:407
  59.2 21.7 %collective-permute-start.9 = (bf16[192,2048]{1,0:T(8,128)(2,1)S(1)}, bf16[192,2048]{1,0:T(8,128)(2,1)S(1)}, u32[]{:S(2)}, u32[]{:S(2)}) collective-permute-start(bf16[192,2048]{1,0:T(8,128)(2,1)S(1)} %collective-permute-done.1.refs_3_), channel_id=1, source_target_pairs={{0,32},{32,0},{1,33},{33,1},{2,34},{34,2},{3,35},{35,3},{4,36},{36... | collective-permute-start | bytes 2359304 | tf_op jit(solution)/shard_map/ppermute | solution.py:407
  74.7 6.2 %collective-permute-start.10 = (bf16[192,2048]{1,0:T(8,128)(2,1)S(1)}, bf16[192,2048]{1,0:T(8,128)(2,1)S(1)}, u32[]{:S(2)}, u32[]{:S(2)}) collective-permute-start(bf16[192,2048]{1,0:T(8,128)(2,1)S(1)} %collective-permute-done.2.refs_4_), channel_id=1, source_target_pairs={{0,32},{32,0},{1,33},{33,1},{2,34},{34,2},{3,35},{35,3},{4,36},{36... | collective-permute-start | bytes 2359304 | tf_op jit(solution)/shard_map/ppermute | solution.py:407
  79.0 4.1 %collective-permute-start.11 = (bf16[192,2048]{1,0:T(8,128)(2,1)S(1)}, bf16[192,2048]{1,0:T(8,128)(2,1)}, u32[]{:S(2)}, u32[]{:S(2)}) collective-permute-start(bf16[192,2048]{1,0:T(8,128)(2,1)S(1)} %collective-permute-done.4.refs_5_), channel_id=1, source_target_pairs={{0,32},{32,0},{1,33},{33,1},{2,34},{34,2},{3,35},{35,3},{4,36},{36... | collective-permute-start | bytes 2359304 | tf_op jit(solution)/shard_map/ppermute | solution.py:407
  105.3 7.8 %collective-permute-start.14 = (bf16[384,5632]{1,0:T(8,128)(2,1)}, bf16[384,5632]{1,0:T(8,128)(2,1)}, u32[]{:S(2)}, u32[]{:S(2)}) collective-permute-start(bf16[384,5632]{1,0:T(8,128)(2,1)} %get-tuple-element.34.packed_a), channel_id=1, source_target_pairs={{0,32},{32,0},{1,33},{33,1},{2,34},{34,2},{3,35},{35,3},{4,36},{36... | collective-permute-start | bytes 12976136 | tf_op jit(solution)/shard_map/ppermute | solution.py:407
  105.4 79.7 %all-to-all-start.1 = ((bf16[32,24,2048]{2,1,0:T(8,128)(2,1)}), bf16[32,24,2048]{2,1,0:T(8,128)(2,1)}, u32[]{:S(2)}, u32[]{:S(2)}) async-start(bf16[32,24,2048]{2,1,0:T(8,128)(2,1)} %bitcast.10), calls=%async_computation.1 | async-start | bytes 6291456 | tf_op jit(solution)/shard_map/all_to_all | solution.py:410
  119.5 21.9 %collective-permute-start.15 = (bf16[384,1024]{1,0:T(8,128)(2,1)}, bf16[384,1024]{1,0:T(8,128)(2,1)S(1)}, u32[]{:S(2)}, u32[]{:S(2)}) collective-permute-start(bf16[384,1024]{1,0:T(8,128)(2,1)} %get-tuple-element.39), channel_id=1, source_target_pairs={{0,192},{64,0},{128,64},{192,128},{1,193},{65,1},{129,65},{193,129... | collective-permute-start | bytes 2359304 | tf_op jit(solution)/shard_map/ppermute | solution.py:404
  120.3 22.6 %collective-permute-start.19 = (bf16[384,1024]{1,0:T(8,128)(2,1)}, bf16[384,1024]{1,0:T(8,128)(2,1)S(1)}, u32[]{:S(2)}, u32[]{:S(2)}) collective-permute-start(bf16[384,1024]{1,0:T(8,128)(2,1)} %get-tuple-element.43), channel_id=1, source_target_pairs={{0,64},{64,128},{128,192},{192,0},{1,65},{65,129},{129,193},{193,1... | collective-permute-start | bytes 2359304 | tf_op jit(solution)/shard_map/ppermute | solution.py:404
  122.8 35.4 %collective-permute-start.17 = (bf16[384,1024]{1,0:T(8,128)(2,1)}, bf16[384,1024]{1,0:T(8,128)(2,1)S(1)}, u32[]{:S(2)}, u32[]{:S(2)}) collective-permute-start(bf16[384,1024]{1,0:T(8,128)(2,1)} %get-tuple-element.40), channel_id=1, source_target_pairs={{0,192},{64,0},{128,64},{192,128},{1,193},{65,1},{129,65},{193,129... | collective-permute-start | bytes 2359304 | tf_op jit(solution)/shard_map/ppermute | solution.py:404
  122.8 35.4 %collective-permute-start.18 = (bf16[384,1024]{1,0:T(8,128)(2,1)}, bf16[384,1024]{1,0:T(8,128)(2,1)S(1)}, u32[]{:S(2)}, u32[]{:S(2)}) collective-permute-start(bf16[384,1024]{1,0:T(8,128)(2,1)} %get-tuple-element.41), channel_id=1, source_target_pairs={{0,64},{64,128},{128,192},{192,0},{1,65},{65,129},{129,193},{193,1... | collective-permute-start | bytes 2359304 | tf_op jit(solution)/shard_map/ppermute | solution.py:404
  142.8 31.5 %collective-permute-start.16 = (bf16[384,1024]{1,0:T(8,128)(2,1)S(1)}, bf16[384,1024]{1,0:T(8,128)(2,1)S(1)}, u32[]{:S(2)}, u32[]{:S(2)}) collective-permute-start(bf16[384,1024]{1,0:T(8,128)(2,1)S(1)} %add.6), channel_id=1, source_target_pairs={{0,192},{64,0},{128,64},{192,128},{1,193},{65,1},{129,65},{193,129... | collective-permute-start | bytes 2359304 | tf_op jit(solution)/shard_map/ppermute | solution.py:404
  144.5 29.8 %collective-permute-start.20 = (bf16[384,1024]{1,0:T(8,128)(2,1)S(1)}, bf16[384,1024]{1,0:T(8,128)(2,1)}, u32[]{:S(2)}, u32[]{:S(2)}) collective-permute-start(bf16[384,1024]{1,0:T(8,128)(2,1)S(1)} %add.7), channel_id=1, source_target_pairs={{0,64},{64,128},{128,192},{192,0},{1,65},{65,129},{129,193},{193,1... | collective-permute-start | bytes 2359304 | tf_op jit(solution)/shard_map/ppermute | solution.py:404
  (19 other events, 378.0 us)
